TPU v7x, 128 devices: a whole 4x4x4 slice. The times are simulated.
128 devices in a mesh: owner: 16 (over z, y), kv: 8 (over x, core).
Axes of the slice: x: 4, y: 4, z: 4, core: 2. Of those that a mesh axis runs over, the one named last changes fastest.
Arguments:
- queries: bfloat16 [512, 8192], P('owner', 'kv'), may hold values from -4.5 to 4.5
- prefix_cache: bfloat16 [16, 8192, 8, 256], P('owner', None, 'kv'), may hold values from -8 to 8
- suffix_cache: bfloat16 [512, 1024, 8, 256], P('owner', None, 'kv'), may hold values from -8 to 8
- suffix_len: int32 [512], P('owner'), may hold values from 1 to 1024, 393216 in all
- fork_prefix: int32 [512, 1], P('owner'), may hold values from 0 to 15; in each aligned block of 32 rows (0 to 31, 32 to 63, ...) at most 4 rows name the same one
- prefix_slot: int32 [16], replicated, may hold values from 0 to 15, each once
- out_weight: bfloat16 [8192, 8192], P('kv', 'owner'), may hold values from -0.375 to 0.375
Outputs:
- projected: bfloat16 [512, 8192], P('kv', 'owner')
Inputs may be any that keep to these rules, and one draw needn't show every extreme that they name: `fork_prefix`: within the 32 rows of one owner index no prefix id appears more than 4 times, and on some owner index one appears exactly 4 times; every prefix id appears on some row. `prefix_slot`: each stored row is named by exactly one prefix id.
All inputs are finite; a program needn't handle non-finite values. No bound on the sum of `suffix_len` on one device may be relied on, other than what follows from the above.
Results may differ from a plain program's by a relative error of at most 0.019.
Values may be sent and summed in bfloat16 or wider, within the bound.
No kernel may reach another device: no remote copies, remote signals or barrier semaphores. Data moves between devices by JAX's collectives and lax.ppermute only.
A program may use at most 192 MiB of HBM per device.

v0:
```python
import jax
import jax.numpy as jnp
from jax import lax
from jax.sharding import PartitionSpec as P


def prefix_partial(received, prefix_cache, group_size, score_scale):
    owners, pre_local, capacity, feature_width = received.shape
    kv_local = prefix_cache.shape[2]
    head_dim = prefix_cache.shape[3] // 2
    query_block = received.reshape(owners, pre_local, capacity, kv_local, group_size, head_dim)
    query_block = query_block.transpose(1, 3, 0, 2, 4, 5).reshape(
        pre_local, kv_local, owners * capacity * group_size, head_dim
    )
    scores = (
        jnp.einsum(
            "pgqd,pkgd->pgqk",
            query_block,
            prefix_cache[..., :head_dim],
            preferred_element_type=jnp.float32,
        )
        * score_scale
    )
    highest = jnp.max(scores, axis=-1)
    weights = jnp.exp(scores - highest[..., None])
    totals = jnp.sum(weights, axis=-1)
    summed = jnp.einsum(
        "pgqk,pkgd->pgqd",
        weights.astype(jnp.bfloat16),
        prefix_cache[..., head_dim:],
        preferred_element_type=jnp.float32,
    )
    stat_shape = (pre_local, kv_local, owners, capacity, group_size)
    summed = (
        summed.reshape(stat_shape + (head_dim,))
        .transpose(2, 0, 3, 1, 4, 5)
        .reshape(owners, pre_local, capacity, feature_width)
    )
    highest = (
        highest.reshape(stat_shape)
        .transpose(2, 0, 3, 1, 4)
        .reshape(owners, pre_local, capacity, kv_local * group_size)
    )
    totals = (
        totals.reshape(stat_shape)
        .transpose(2, 0, 3, 1, 4)
        .reshape(owners, pre_local, capacity, kv_local * group_size)
    )
    return (summed, highest, totals)


def combine_parts(summed_pre, top_pre, total_pre, summed_suf, top_suf, total_suf, head_dim):
    leading = top_pre.shape
    top_all = jnp.maximum(top_pre, top_suf)
    factor_pre = jnp.exp(top_pre - top_all)
    factor_suf = jnp.exp(top_suf - top_all)
    numerator = (
        summed_pre.reshape(leading + (head_dim,)) * factor_pre[..., None]
        + summed_suf.reshape(leading + (head_dim,)) * factor_suf[..., None]
    )
    denominator = total_pre * factor_pre + total_suf * factor_suf
    return (numerator / denominator[..., None]).reshape(summed_pre.shape).astype(jnp.bfloat16)


def body(queries, prefix_cache, suffix_cache, suffix_len, fork_prefix, prefix_slot, out_weight):
    rows_dev, feature_width = queries.shape
    kv_local = prefix_cache.shape[2]
    head_dim = prefix_cache.shape[3] // 2
    group_size = feature_width // (kv_local * head_dim)
    head_count = kv_local * group_size
    owners = lax.axis_size("owner")
    prefixes = prefix_slot.shape[0]
    pre_local = prefixes // owners
    capacity = max(2, 2 * rows_dev // prefixes)
    slot_count = prefixes * capacity
    score_scale = head_dim ** (-0.5)
    row_ids = jnp.arange(rows_dev, dtype=jnp.int32)
    picked = fork_prefix[:, 0][:, None] == jnp.arange(prefixes, dtype=jnp.int32)[None, :]
    stored = jnp.sum(jnp.where(picked, prefix_slot[None, :], 0), axis=1)
    same_slot = stored[:, None] == stored[None, :]
    row_rank = jnp.sum(same_slot & (row_ids[None, :] < row_ids[:, None]), axis=1)
    target = stored * capacity + row_rank
    matches = target[None, :] == jnp.arange(slot_count, dtype=jnp.int32)[:, None]
    anchor = jnp.sum(jnp.where(matches, row_ids[None, :], 0), axis=1)
    filled = jnp.any(matches, axis=1)
    query_rows = queries.reshape(rows_dev, kv_local, group_size, head_dim)
    suffix_scores = (
        jnp.einsum(
            "rgjd,rsgd->rgjs",
            query_rows,
            suffix_cache[..., :head_dim],
            preferred_element_type=jnp.float32,
        )
        * score_scale
    )
    live_mask = (jnp.arange(suffix_cache.shape[1], dtype=jnp.int32)[None, :] < suffix_len[:, None])[
        :, None, None, :
    ]
    masked = jnp.where(live_mask, suffix_scores, -1e30)
    top_suf = jnp.max(masked, axis=-1)
    weights_suf = jnp.where(live_mask, jnp.exp(masked - top_suf[..., None]), 0.0)
    total_suf = jnp.sum(weights_suf, axis=-1).reshape(rows_dev, head_count)
    summed_suf = jnp.einsum(
        "rgjs,rsgd->rgjd",
        weights_suf.astype(jnp.bfloat16),
        suffix_cache[..., head_dim:],
        preferred_element_type=jnp.float32,
    ).reshape(rows_dev, feature_width)
    top_suf = top_suf.reshape(rows_dev, head_count)
    taken = jnp.take(queries, anchor, axis=0)
    kept = jnp.where(
        filled.reshape((slot_count,) + (1,) * (queries.ndim - 1)), taken, jnp.zeros_like(taken)
    )
    outgoing = kept.reshape((owners, pre_local, capacity) + queries.shape[1:])
    received = lax.all_to_all(outgoing, "owner", split_axis=0, concat_axis=0, tiled=True)
    summed_pre, top_pre, total_pre = prefix_partial(received, prefix_cache, group_size, score_scale)
    summed_pre, top_pre, total_pre = (
        lax.all_to_all(summed_pre, "owner", split_axis=0, concat_axis=0, tiled=True),
        lax.all_to_all(top_pre, "owner", split_axis=0, concat_axis=0, tiled=True),
        lax.all_to_all(total_pre, "owner", split_axis=0, concat_axis=0, tiled=True),
    )
    attended = combine_parts(
        jnp.take(summed_pre.reshape(slot_count, feature_width), target, axis=0),
        jnp.take(top_pre.reshape(slot_count, head_count), target, axis=0),
        jnp.take(total_pre.reshape(slot_count, head_count), target, axis=0),
        summed_suf,
        top_suf,
        total_suf,
        head_dim,
    )
    partial_value = jnp.dot(
        lax.all_gather(attended, "owner", axis=0, tiled=True),
        out_weight,
        preferred_element_type=jnp.float32,
    )
    return lax.psum_scatter(
        partial_value.astype(jnp.bfloat16), "kv", scatter_dimension=0, tiled=True
    )


def solution(mesh):
    placed = (
        P("owner", "kv"),
        P("owner", None, "kv", None),
        P("owner", None, "kv", None),
        P("owner"),
        P("owner", None),
        P(),
        P("kv", "owner"),
    )
    return jax.shard_map(
        body, mesh=mesh, in_specs=placed, out_specs=P("kv", "owner"), check_vma=False
    )
```

profile of v0, /device:TPU:0, one launch (start us, length us, event | category | flops | bytes accessed | tf_op | source)
XLA Modules:
  0.0 172.1 jit_solution(15734140412349688825)
XLA Ops:
  6.5 0.0 copy-start
  6.5 0.8 select_reduce_fusion.1
  7.4 0.2 convert_reduce_fusion
  7.6 0.1 select_reduce_fusion
  7.7 0.1 reduce_sum.52
  7.8 0.1 fusion.25
  7.9 1.6 gather_fusion
  9.5 0.1 gather.14
  9.6 0.1 broadcast_in_dim.104
  9.7 0.8 fusion.21
  10.5 8.1 %all-to-all-start = ((bf16[16,1,4,1024]{3,2,1,0:T(4,128)(2,1)}), bf16[16,1,4,1024]{3,2,1,0:T(4,128)(2,1)S(1)}, u32[]{:S(2)}, u32[]{:S(2)}) async-start(bf16[16,1,4,1024]{3,2,1,0:T(4,128)(2,1)} %fusion.21), calls=%async_computation | async-start | bytes 262144 | tf_op jit(solution)/shard_map/all_to_all | solution.py:115
  18.7 0.7 iota_compare_fusion
  19.4 0.9 copy.24
  20.3 5.7 %fusion.33 = (f32[32,8]{1,0:T(8,128)S(1)}, f32[32,8,1024]{2,1,0:T(8,128)S(1)}) fusion(bf16[32,8,128]{2,1,0:T(8,128)(2,1)S(1)} %bitcast.71, bf16[32,1024,1,256]{3,1,0,2:T(8,128)(2,1)} %bitcast.64, pred[32,1024]{1,0:T(8,128)(4,1)S(1)} %iota_compare_fusion), kind=kOutput, calls=%fused_computation.63 | convolution fusion | flops 67895040 | bytes 9536512 | tf_op jit(solution)/shard_map/rgjd,rsgd->rgjs/dot_general | solution.py:88
  26.0 0.4 fusion.14
  26.4 0.2 all-to-all-done
  26.6 0.1 reshape.197
  26.7 9.7 %multiply_reduce_fusion = (f32[512]{0:T(512)S(1)}, f32[512,8192]{1,0:T(8,128)}) fusion(bf16[512,128]{1,0:T(8,128)(2,1)S(1)} %reshape.197, bf16[1,8192,1,256]{3,1,2,0:T(8,128)(2,1)} %param.10), kind=kOutput, calls=%fused_computation.5 | convolution fusion | flops 1082129920 | bytes 19007488 | tf_op jit(solution)/shard_map/pgqd,pkgd->pgqk/dot_general | solution.py:16
  36.3 8.6 %fusion = f32[512]{0:T(512)S(1)} fusion(f32[512,8192]{1,0:T(8,128)} %get-tuple-element.12, f32[512]{0:T(512)S(1)} %get-tuple-element.11), kind=kLoop, calls=%fused_computation.6 | loop fusion | flops 12582400 | bytes 16781312 | tf_op jit(solution)/shard_map/reduce_sum | solution.py:26
  45.0 0.7 reshape_transpose_reshape.12
  45.7 7.0 %all-to-all-start.3 = ((f32[16,1,4,8]{3,2,1,0:T(4,128)}), f32[16,1,4,8]{3,2,1,0:T(4,128)S(1)}, u32[]{:S(2)}, u32[]{:S(2)}) async-start(f32[16,1,4,8]{3,2,1,0:T(4,128)} %bitcast.15), calls=%async_computation.3 | async-start | bytes 65536 | tf_op jit(solution)/shard_map/all_to_all | solution.py:120
  52.7 0.7 reshape_transpose_reshape.11
  53.4 6.9 %all-to-all-done.3 = f32[16,1,4,8]{3,2,1,0:T(4,128)S(1)} async-done(((f32[16,1,4,8]{3,2,1,0:T(4,128)}), f32[16,1,4,8]{3,2,1,0:T(4,128)S(1)}, u32[]{:S(2)}, u32[]{:S(2)}) %all-to-all-start.3) | async-done | bytes 2080 | tf_op jit(solution)/shard_map/all_to_all | solution.py:120
  60.3 3.5 %all-to-all-start.2 = ((f32[16,1,4,8]{3,2,1,0:T(4,128)}), f32[16,1,4,8]{3,2,1,0:T(4,128)S(1)}, u32[]{:S(2)}, u32[]{:S(2)}) async-start(f32[16,1,4,8]{3,2,1,0:T(4,128)} %bitcast.9), calls=%async_computation.2 | async-start | bytes 65536 | tf_op jit(solution)/shard_map/all_to_all | solution.py:119
  63.8 8.2 %fusion.4 = f32[512,128]{1,0:T(8,128)S(1)} fusion(f32[512,8192]{1,0:T(8,128)} %get-tuple-element.12, f32[512]{0:T(512)S(1)} %get-tuple-element.11, bf16[1,8192,1,256]{3,1,2,0:T(8,128)(2,1)} %param.10), kind=kOutput, calls=%fused_computation.12 | convolution fusion | flops 1086324736 | bytes 19138560 | tf_op jit(solution)/shard_map/pgqk,pkgd->pgqd/dot_general | solution.py:27
  72.0 0.8 reshape_transpose_reshape.10
  72.8 0.6 gather_fusion.3
  73.4 0.0 all-to-all-done.2
  73.4 7.2 %all-to-all-start.1 = ((f32[16,1,4,1024]{3,2,1,0:T(4,128)}), f32[16,1,4,1024]{3,2,1,0:T(4,128)S(1)}, u32[]{:S(2)}, u32[]{:S(2)}) async-start(f32[16,1,4,1024]{3,2,1,0:T(4,128)} %bitcast.6), calls=%async_computation.1 | async-start | bytes 524288 | tf_op jit(solution)/shard_map/all_to_all | solution.py:118
  80.5 0.0 all-gather.2.cloned.1.call-start
  80.6 0.6 gather_fusion.2
  81.2 0.1 fusion.24
  81.3 4.7 %fusion.13 = f32[32,8,128]{2,1,0:T(8,128)S(1)} fusion(bf16[32,1024,1,256]{3,1,0,2:T(8,128)(2,1)} %bitcast.65, f32[32,8,1024]{2,1,0:T(8,128)S(1)} %get-tuple-element.14, f32[32,8]{1,0:T(8,128)S(1)} %get-tuple-element.13, pred[32,1024]{1,0:T(8,128)(4,1)S(1)} %iota_compare_fusion, f32[32,8]{1,0:T(8,128)S(1)} %get-tuple-element.9), kind=kOutput, calls=%fused_computation.21 | convolution fusion | flops 67928064 | bytes 9603072 | tf_op jit(solution)/shard_map/rgjs,rsgd->rgjd/dot_general | solution.py:103
  85.9 3.3 %all-to-all-done.1 = f32[16,1,4,1024]{3,2,1,0:T(4,128)S(1)} async-done(((f32[16,1,4,1024]{3,2,1,0:T(4,128)}), f32[16,1,4,1024]{3,2,1,0:T(4,128)S(1)}, u32[]{:S(2)}, u32[]{:S(2)}) %all-to-all-start.1) | async-done | bytes 262176 | tf_op jit(solution)/shard_map/all_to_all | solution.py:118
  89.2 0.1 reshape.200
  89.3 0.6 gather_fusion.1
  89.9 0.1 mul.69
  90.0 0.1 div.11
  90.1 0.7 fusion.20
  90.9 0.0 all-gather.2.cloned.1.call-update
  90.9 0.0 reduce-scatter.2.cloned.1.call-start
  91.0 41.3 %all-gather.2.cloned.1.call-done = bf16[512,1024]{1,0:T(8,128)(2,1)} async-done(((bf16[32,1024]{1,0:T(8,128)(2,1)}), bf16[512,1024]{1,0:T(8,128)(2,1)}) %all-gather.2.cloned.1.call-update) | async-done | bytes 1048592 | tf_op jit(solution)/shard_map/all_gather | solution.py:132
  132.2 0.0 copy-done
  132.2 2.8 %convolution_convert_fusion = bf16[512,512]{1,0:T(8,128)(2,1)} fusion(bf16[512,1024]{1,0:T(8,128)(2,1)} %all-gather.2.cloned.1.call-done, bf16[1024,512]{1,0:T(8,128)(2,1)S(1)} %copy-done), kind=kOutput, calls=%fused_computation.19 | convolution fusion | flops 537133056 | bytes 2621440 | tf_op jit(solution)/shard_map/dot_general | solution.py:131
  135.0 0.0 reduce-scatter.2.cloned.1.call-update
  135.0 30.3 %reduce-scatter.2.cloned.1.call-done = bf16[64,512]{1,0:T(8,128)(2,1)} async-done(((bf16[512,512]{1,0:T(8,128)(2,1)}), bf16[64,512]{1,0:T(8,128)(2,1)}) %reduce-scatter.2.cloned.1.call-update) | async-done | bytes 65552 | tf_op jit(solution)/shard_map/reduce_scatter | solution.py:136
  (8 shorter events, 0.1 us)
Async XLA Ops:
  6.5 125.7 %copy-start = (bf16[1024,512]{1,0:T(8,128)(2,1)S(1)}, bf16[1024,512]{1,0:T(8,128)(2,1)}, u32[]{:S(2)}) copy-start(bf16[1024,512]{1,0:T(8,128)(2,1)} %param.15) | copy-start | bytes 3145732
  10.5 16.1 %all-to-all-start = ((bf16[16,1,4,1024]{3,2,1,0:T(4,128)(2,1)}), bf16[16,1,4,1024]{3,2,1,0:T(4,128)(2,1)S(1)}, u32[]{:S(2)}, u32[]{:S(2)}) async-start(bf16[16,1,4,1024]{3,2,1,0:T(4,128)(2,1)} %fusion.21), calls=%async_computation | async-start | bytes 262144 | tf_op jit(solution)/shard_map/all_to_all | solution.py:115
  45.7 14.6 %all-to-all-start.3 = ((f32[16,1,4,8]{3,2,1,0:T(4,128)}), f32[16,1,4,8]{3,2,1,0:T(4,128)S(1)}, u32[]{:S(2)}, u32[]{:S(2)}) async-start(f32[16,1,4,8]{3,2,1,0:T(4,128)} %bitcast.15), calls=%async_computation.3 | async-start | bytes 65536 | tf_op jit(solution)/shard_map/all_to_all | solution.py:120
  60.3 13.0 %all-to-all-start.2 = ((f32[16,1,4,8]{3,2,1,0:T(4,128)}), f32[16,1,4,8]{3,2,1,0:T(4,128)S(1)}, u32[]{:S(2)}, u32[]{:S(2)}) async-start(f32[16,1,4,8]{3,2,1,0:T(4,128)} %bitcast.9), calls=%async_computation.2 | async-start | bytes 65536 | tf_op jit(solution)/shard_map/all_to_all | solution.py:119
  73.4 15.9 %all-to-all-start.1 = ((f32[16,1,4,1024]{3,2,1,0:T(4,128)}), f32[16,1,4,1024]{3,2,1,0:T(4,128)S(1)}, u32[]{:S(2)}, u32[]{:S(2)}) async-start(f32[16,1,4,1024]{3,2,1,0:T(4,128)} %bitcast.6), calls=%async_computation.1 | async-start | bytes 524288 | tf_op jit(solution)/shard_map/all_to_all | solution.py:118
  80.5 51.7 %all-gather.2.cloned.1.call-start = ((), (), s32[]{:S(2)}) async-start(), calls=%async_computation.5 | async-start | bytes 1114112 | tf_op jit(solution)/shard_map/all_gather | solution.py:132
  90.9 74.4 %reduce-scatter.2.cloned.1.call-start = ((), (), s32[]{:S(2)}) async-start(), calls=%async_computation.6 | async-start | bytes 589824 | tf_op jit(solution)/shard_map/reduce_scatter | solution.py:136
Sparse Core Ops, SparseCore 0:
  91.0 41.1 all-gather.1
  135.1 30.1 reduce-scatter.1
where the time goes:
time: 173 us; the launch traced here: 172 us
  waiting for transfers between devices  82 us (47%)
  matrix products  31 us (18%)
  starting transfers between devices  25.9 us (15%)
  between operations  13.6 us (8%)
  other arithmetic  12.7 us (7%)
  local copies, waits for them, and re-layouts  7.03 us (4%)
    all_gather x1, waiting for transfers between devices, body(): lax.all_gather(attended, 'owner', axis=0, tiled=True)  41.3 us
    reduce_scatter x1, waiting for transfers between devices, body(): lax.psum_scatter(partial_value.astype(jnp.bfloat16), 'kv', scatter_dimens...  30.3 us
    dot_general x1, matrix products, prefix_partial(): jnp.einsum('pgqd,pkgd->pgqk', query_block, prefix_cache[..., :head_dim],...  9.65 us
    reduce_sum x1, other arithmetic, prefix_partial(): totals = jnp.sum(weights, axis=-1)  8.62 us
    dot_general x1, matrix products, prefix_partial(): jnp.einsum('pgqk,pkgd->pgqd', weights.astype(jnp.bfloat16), prefix_cache[...  8.19 us
    all_to_all x1, starting transfers between devices, body(): lax.all_to_all(outgoing, 'owner', split_axis=0, concat_axis=0, tiled=True)  8.13 us
    all_to_all x1, starting transfers between devices, body(): lax.all_to_all(summed_pre, 'owner', split_axis=0, concat_axis=0, tiled=True)  7.16 us
    all_to_all x1, starting transfers between devices, body(): lax.all_to_all(total_pre, 'owner', split_axis=0, concat_axis=0, tiled=True)  7.02 us
  transfers between devices with their start and end apart: 6, of which 5 were waited for; matrix products, arithmetic and copies ran while one was open for 14% of the time, Pallas kernels for 0%

commit v1 on v0

v1 whole, which is shorter than its diff:
```python
import functools

import jax
import jax.numpy as jnp
from jax import lax
from jax.experimental import pallas as pl
from jax.experimental.pallas import tpu as pltpu
from jax.sharding import PartitionSpec as P

LOG2E = 1.4426950408889634
NT = (((1,), (1,)), ((), ()))
VMEM = pl.BlockSpec(memory_space=pltpu.VMEM)
SMEM = pl.BlockSpec(memory_space=pltpu.SMEM)
ANY = pl.BlockSpec(memory_space=pl.ANY)
MIB = 2**20


def one_hot_slots(fork_ref, slot_ref, capacity):
    rows = fork_ref.shape[1]
    prefixes = slot_ref.shape[1]
    sub = lax.broadcasted_iota(jnp.int32, (rows, rows), 0)
    lane = lax.broadcasted_iota(jnp.int32, (rows, rows), 1)
    eye = sub == lane
    fork_row = jnp.broadcast_to(fork_ref[...], (rows, rows))
    fork_col = jnp.sum(jnp.where(eye, fork_row, 0), axis=1, keepdims=True)
    picked = fork_col == lax.broadcasted_iota(jnp.int32, (rows, prefixes), 1)
    slots_all = jnp.broadcast_to(slot_ref[...], (rows, prefixes))
    stored_col = jnp.sum(jnp.where(picked, slots_all, 0), axis=1, keepdims=True)
    stored_row = jnp.sum(
        jnp.where(eye, jnp.broadcast_to(stored_col, (rows, rows)), 0), axis=0, keepdims=True
    )
    earlier = (stored_col == stored_row) & (sub < lane)
    rank_row = jnp.sum(earlier.astype(jnp.int32), axis=0, keepdims=True)
    target = stored_row * capacity + rank_row
    count = prefixes * capacity
    return lax.broadcasted_iota(jnp.int32, (count, rows), 0) == target


def route_kernel(fork_ref, slot_ref, query_ref, out_ref, *, capacity):
    hot = one_hot_slots(fork_ref, slot_ref, capacity).astype(jnp.bfloat16)
    out_ref[...] = jnp.dot(hot, query_ref[...], preferred_element_type=jnp.float32).astype(
        jnp.bfloat16
    )


def suffix_kernel(len_ref, q_ref, kv_hbm, out_ref, lse_ref, kv, sems, q_s, o_s, *, group, scale):
    rows, keys, width = kv.shape
    hd = width // 2
    heads = q_ref.shape[1] // hd
    c2 = scale * LOG2E

    def copy_of(r):
        return pltpu.make_async_copy(kv_hbm.at[r], kv.at[r], sems.at[r])

    def issue(r, carry):
        copy_of(r).start()
        return carry

    lax.fori_loop(0, rows, issue, 0)
    for h in range(heads):
        q_s[pl.ds(h, rows, stride=heads), :] = q_ref[:, h * hd : (h + 1) * hd].astype(jnp.float32)
    span = group * heads

    def step(g, carry):
        def wait(i, c):
            copy_of(g * group + i).wait()
            return c

        lax.fori_loop(0, group, wait, 0)
        row_id = lax.broadcasted_iota(jnp.int32, (span, 1), 0) // heads
        length = jnp.zeros((span, 1), jnp.int32)
        for i in range(group):
            length = jnp.where(row_id == i, len_ref[g * group + i], length)
        base = pl.multiple_of(g * span, span)
        s = jnp.concatenate(
            [
                lax.dot_general(
                    q_s[pl.ds(base + i * heads, heads), :].astype(jnp.bfloat16),
                    kv[g * group + i, :, :hd],
                    NT,
                    preferred_element_type=jnp.float32,
                )
                for i in range(group)
            ],
            axis=0,
        )
        live = lax.broadcasted_iota(jnp.int32, (span, keys), 1) < length
        s = jnp.where(live, s, -1e30)
        m = jnp.max(s, axis=-1, keepdims=True)
        p = jnp.where(live, jnp.exp2((s - m) * c2), 0.0)
        total = jnp.sum(p, axis=-1, keepdims=True)
        o = jnp.concatenate(
            [
                jnp.dot(
                    p[i * heads : (i + 1) * heads].astype(jnp.bfloat16),
                    kv[g * group + i, :, hd:],
                    preferred_element_type=jnp.float32,
                )
                for i in range(group)
            ],
            axis=0,
        )
        o_s[pl.ds(base, span), :] = o / total
        lse_ref[pl.ds(base, span), :] = jnp.broadcast_to(m * c2 + jnp.log2(total), (span, hd))
        return carry

    lax.fori_loop(0, rows // group, step, 0)
    for h in range(heads):
        out_ref[:, h * hd : (h + 1) * hd] = o_s[pl.ds(h, rows, stride=heads), :]


def prefix_kernel(x_ref, kv_hbm, out_ref, kv, sems, q_s, m_s, acc_s, vt_s, *, kb, ct, scale, ahead):
    keys = kv.shape[0]
    hd = kv.shape[1] // 2
    slots = x_ref.shape[0]
    feat = x_ref.shape[1]
    heads = feat // hd
    n = keys // kb
    count = slots * heads
    c2 = scale * LOG2E

    def copy_of(c):
        part = pl.ds(c * kb, kb)
        return pltpu.make_async_copy(kv_hbm.at[part], kv.at[part], sems.at[c])

    for c in range(min(ahead, n)):
        copy_of(c).start()
    qf = jnp.concatenate([x_ref[:, h * hd : (h + 1) * hd] for h in range(heads)], axis=0)
    qf = qf.astype(jnp.float32).T * c2
    hi = qf.astype(jnp.bfloat16)
    q_s[:hd, :] = hi
    q_s[hd:, :] = (qf - hi.astype(jnp.float32)).astype(jnp.bfloat16)
    vt_s[hd:, :] = jnp.ones((vt_s.shape[0] - hd, kb), jnp.bfloat16)

    def scores(c, t):
        k = kv[c * kb : (c + 1) * kb, :hd]
        return jnp.dot(
            jnp.concatenate([k, k], axis=1),
            q_s[:, t * ct : (t + 1) * ct],
            preferred_element_type=jnp.float32,
        )

    items = [(c, t) for c in range(n) for t in range(count // ct)]
    copy_of(0).wait()
    s_next = scores(*items[0])
    for idx, (c, t) in enumerate(items):
        s = s_next
        if idx + 1 < len(items):
            c1, t1 = items[idx + 1]
            if t1 == 0:
                copy_of(c1).wait()
                if c1 + ahead - 1 < n:
                    copy_of(c1 + ahead - 1).start()
            s_next = scores(c1, t1)
        if t == 0:
            vt_s[:hd, :] = kv[c * kb : (c + 1) * kb, hd:].T
        cols = slice(t * ct, (t + 1) * ct)
        m_new = jnp.max(s, axis=0, keepdims=True)
        if c > 0:
            m_old = m_s[:1, cols]
            m_new = jnp.maximum(m_old, m_new)
        p = jnp.exp2(s - m_new)
        o = jnp.dot(vt_s[...], p.astype(jnp.bfloat16), preferred_element_type=jnp.float32)
        if c > 0:
            o = o + jnp.exp2(m_old - m_new) * acc_s[:, cols]
        m_s[:, cols] = jnp.broadcast_to(m_new, (8, ct))
        acc_s[:, cols] = o
    total = acc_s[hd : hd + 1, :]
    out = (acc_s[:hd, :] / total).T.astype(jnp.bfloat16)
    lse = jnp.broadcast_to(m_s[:1, :] + jnp.log2(total), (hd, count)).T
    lane = lax.broadcasted_iota(jnp.int32, (slots, hd), 1)
    pieces = jnp.zeros((slots, hd), jnp.float32)
    for h in range(heads):
        out_ref[:, h * hd : (h + 1) * hd] = out[h * slots : (h + 1) * slots, :]
        rest = lse[h * slots : (h + 1) * slots, :]
        for j in range(3):
            part = rest.astype(jnp.bfloat16).astype(jnp.float32)
            rest = rest - part
            pieces = jnp.where(lane == j * heads + h, part, pieces)
    out_ref[:, feat:] = pieces.astype(jnp.bfloat16)


def combine_kernel(fork_ref, slot_ref, recv_ref, osuf_ref, lsuf_ref, out_ref, *, capacity, heads):
    rows, feat = osuf_ref.shape
    hd = feat // heads
    copies = out_ref.shape[0]
    hot = one_hot_slots(fork_ref, slot_ref, capacity).astype(jnp.float32).T.astype(jnp.bfloat16)
    got = jnp.dot(hot, recv_ref[...], preferred_element_type=jnp.float32)
    for h in range(heads):
        cols = slice(h * hd, (h + 1) * hd)
        lse_pre = (
            got[:, feat + h : feat + h + 1]
            + got[:, feat + heads + h : feat + heads + h + 1]
            + got[:, feat + 2 * heads + h : feat + 2 * heads + h + 1]
        )
        lse_pre = jnp.broadcast_to(lse_pre, (rows, hd))
        lse_suf = lsuf_ref[pl.ds(h, rows, stride=heads), :]
        top = jnp.maximum(lse_pre, lse_suf)
        a = jnp.exp2(lse_pre - top)
        b = jnp.exp2(lse_suf - top)
        value = ((a * got[:, cols] + b * osuf_ref[:, cols]) / (a + b)).astype(jnp.bfloat16)
        for i in range(copies):
            out_ref[i, :, cols] = value


def body(queries, prefix_cache, suffix_cache, suffix_len, fork_prefix, prefix_slot, out_weight):
    rows, feat = queries.shape
    keys = prefix_cache.shape[1]
    hd = prefix_cache.shape[3] // 2
    heads = feat // hd
    owners = lax.axis_size("owner")
    prefixes = prefix_slot.shape[0]
    capacity = max(2, 2 * rows // prefixes)
    slots = prefixes * capacity
    scale = hd**-0.5
    fork_row = fork_prefix.reshape(1, rows)
    slot_row = prefix_slot.reshape(1, prefixes)
    limit = pltpu.CompilerParams(vmem_limit_bytes=56 * MIB)

    outgoing = pl.pallas_call(
        functools.partial(route_kernel, capacity=capacity),
        out_shape=jax.ShapeDtypeStruct((slots, feat), jnp.bfloat16),
        in_specs=[VMEM, VMEM, VMEM],
        out_specs=VMEM,
        name="route",
    )(fork_row, slot_row, queries)
    received = lax.all_to_all(
        outgoing.reshape(owners, capacity, feat), "owner", split_axis=0, concat_axis=0, tiled=True
    )

    suffix_keys = suffix_cache.shape[1]
    o_suf, lse_suf = pl.pallas_call(
        functools.partial(suffix_kernel, group=8, scale=scale),
        out_shape=(
            jax.ShapeDtypeStruct((rows, feat), jnp.float32),
            jax.ShapeDtypeStruct((rows * heads, hd), jnp.float32),
        ),
        in_specs=[SMEM, VMEM, ANY],
        out_specs=(VMEM, VMEM),
        scratch_shapes=[
            pltpu.VMEM((rows, suffix_keys, 2 * hd), jnp.bfloat16),
            pltpu.SemaphoreType.DMA((rows,)),
            pltpu.VMEM((rows * heads, hd), jnp.float32),
            pltpu.VMEM((rows * heads, hd), jnp.float32),
        ],
        compiler_params=limit,
        cost_estimate=pl.CostEstimate(
            flops=4 * rows * heads * suffix_keys * hd,
            bytes_accessed=rows * suffix_keys * 4 * hd,
            transcendentals=rows * heads * suffix_keys,
        ),
        name="suffix",
    )(suffix_len, queries, suffix_cache.reshape(rows, suffix_keys, 2 * hd))

    kb, ct = 2048, 256
    count = slots * heads
    partial = pl.pallas_call(
        functools.partial(prefix_kernel, kb=kb, ct=ct, scale=scale, ahead=3),
        out_shape=jax.ShapeDtypeStruct((slots, feat + hd), jnp.bfloat16),
        in_specs=[VMEM, ANY],
        out_specs=VMEM,
        scratch_shapes=[
            pltpu.VMEM((keys, 2 * hd), jnp.bfloat16),
            pltpu.SemaphoreType.DMA((keys // kb,)),
            pltpu.VMEM((2 * hd, count), jnp.bfloat16),
            pltpu.VMEM((8, count), jnp.float32),
            pltpu.VMEM((hd + 16, count), jnp.float32),
            pltpu.VMEM((hd + 16, kb), jnp.bfloat16),
        ],
        compiler_params=limit,
        cost_estimate=pl.CostEstimate(
            flops=4 * count * keys * hd,
            bytes_accessed=keys * 4 * hd,
            transcendentals=count * keys,
        ),
        name="prefix",
    )(received.reshape(slots, feat), prefix_cache.reshape(keys, 2 * hd))
    returned = lax.all_to_all(
        partial.reshape(owners, capacity, feat + hd),
        "owner",
        split_axis=0,
        concat_axis=0,
        tiled=True,
    )

    attended = pl.pallas_call(
        functools.partial(combine_kernel, capacity=capacity, heads=heads),
        out_shape=jax.ShapeDtypeStruct((owners, rows, feat), jnp.bfloat16),
        in_specs=[VMEM] * 5,
        out_specs=VMEM,
        name="combine",
    )(fork_row, slot_row, returned.reshape(slots, feat + hd), o_suf, lse_suf)
    gathered = lax.all_to_all(attended, "owner", split_axis=0, concat_axis=0, tiled=True)

    members = lax.axis_size("kv")
    chips = members // 2
    place = lax.axis_index("kv")
    chip, core = place // 2, place % 2
    block = owners * rows // members
    cols = out_weight.shape[1]
    full = gathered.reshape(chips, 2, block, feat)
    theirs = jnp.dot(
        lax.dynamic_index_in_dim(full, 1 - core, 1, keepdims=False).reshape(chips * block, feat),
        out_weight,
        preferred_element_type=jnp.float32,
    ).astype(jnp.bfloat16)
    from_pair = lax.ppermute(theirs, "kv", [(i, i ^ 1) for i in range(members)])
    mine = jnp.dot(
        lax.dynamic_index_in_dim(full, core, 1, keepdims=False).reshape(chips * block, feat),
        out_weight,
        preferred_element_type=jnp.float32,
    )
    pair_sum = (mine + from_pair.astype(jnp.float32)).reshape(chips, block, cols)
    pair_sent = pair_sum.astype(jnp.bfloat16)
    total = lax.dynamic_index_in_dim(pair_sum, chip, 0, keepdims=False)
    for d in range(1, chips):
        piece = lax.dynamic_index_in_dim(pair_sent, (chip + d) % chips, 0, keepdims=False)
        moved = lax.ppermute(
            piece,
            "kv",
            [(x * 2 + c, ((x + d) % chips) * 2 + c) for x in range(chips) for c in range(2)],
        )
        total = total + moved.astype(jnp.float32)
    return total.astype(jnp.bfloat16)


def solution(mesh):
    placed = (
        P("owner", "kv"),
        P("owner", None, "kv", None),
        P("owner", None, "kv", None),
        P("owner"),
        P("owner", None),
        P(),
        P("kv", "owner"),
    )
    return jax.shard_map(
        body, mesh=mesh, in_specs=placed, out_specs=P("kv", "owner"), check_vma=False
    )
```

time: 173 us -> 82.6 us (0.48)
  waiting for transfers between devices: 82 us -> 22.4 us
  matrix products: 31 us -> 0.87 us
  Pallas kernels: 0 us -> 22.8 us
  blocking collectives: 0 us -> 15.9 us
  between operations: 13.6 us -> 0.2 us
  other arithmetic: 12.7 us -> 0.69 us
  starting transfers between devices: 25.9 us -> 15.3 us
  local copies, waits for them, and re-layouts: 7.03 us -> 4.02 us
    all_gather x1 -> x0, waiting for transfers between devices: 41.3 us -> none  [body(): lax.all_gather(attended, 'owner', axis=0, tiled=True)]
    reduce_scatter x1 -> x0, waiting for transfers between devices: 30.3 us -> none  [body(): lax.psum_scatter(partial_value.astype(jnp.bfloat16), 'kv', scatter_dimens...]
    dot_general x5 -> x2, matrix products: 31 us -> 0.87 us  [the longest x1 0.43 us: body(): jnp.dot(lax.dynamic_index_in_dim(full, core, 1, keepdims=False).reshape(c...]
    pallas_call x0 -> x4, Pallas kernels: none -> 22.8 us  [the longest x1 9.41 us: body(): pl.pallas_call(functools.partial(prefix_kernel, kb=kb, ct=ct, scale=scale...]
    all_to_all x0 -> x1, blocking collectives: none -> 15.9 us  [body(): lax.all_to_all(outgoing.reshape(owners, capacity, feat), 'owner', split_a...]
    all_to_all x4 -> x2, starting transfers between devices: 25.8 us -> 10.7 us  [the longest x1 7.15 us: body(): lax.all_to_all(attended, 'owner', split_axis=0, concat_axis=0, tiled=True)]
    reduce_sum x5 -> x0, other arithmetic: 10.2 us -> none  [the longest x1 8.62 us: prefix_partial(): totals = jnp.sum(weights, axis=-1)]
    ppermute x0 -> x4, waiting for transfers between devices: none -> 6.52 us  [the longest x3 5.08 us: body(): lax.ppermute(piece, 'kv', [(x * 2 + c, (x + d) % chips * 2 + c) for x in...]
  transfers between devices with their start and end apart: 6 -> 6, of which waited for: 5 -> 5; matrix products, arithmetic and copies ran while one was open for 14% -> 0% of each run, Pallas kernels for 0% -> 10%
where the time goes in v1:
time: 82.6 us; the launch traced here: 82.1 us
  Pallas kernels  22.8 us (28%)
  waiting for transfers between devices  22.4 us (27%)
  blocking collectives  15.9 us (19%)
  starting transfers between devices  15.3 us (19%)
  local copies, waits for them, and re-layouts  4.02 us (5%)
  matrix products  0.87 us (1%)
    all_to_all x1, blocking collectives, body(): lax.all_to_all(outgoing.reshape(owners, capacity, feat), 'owner', split_a...  15.9 us
    all_to_all x1, waiting for transfers between devices, body(): lax.all_to_all(attended, 'owner', split_axis=0, concat_axis=0, tiled=True)  15.8 us
    pallas_call x1, Pallas kernels, body(): pl.pallas_call(functools.partial(prefix_kernel, kb=kb, ct=ct, scale=scale...  9.41 us
    pallas_call x1, Pallas kernels, body(): pl.pallas_call(functools.partial(suffix_kernel, group=8, scale=scale), ou...  8.57 us
    all_to_all x1, starting transfers between devices, body(): lax.all_to_all(attended, 'owner', split_axis=0, concat_axis=0, tiled=True)  7.15 us
    ppermute x3, waiting for transfers between devices, body(): lax.ppermute(piece, 'kv', [(x * 2 + c, (x + d) % chips * 2 + c) for x in...  5.08 us
    ppermute x3, starting transfers between devices, body(): lax.ppermute(piece, 'kv', [(x * 2 + c, (x + d) % chips * 2 + c) for x in...  4.51 us
    all_to_all x1, starting transfers between devices, body(): lax.all_to_all(partial.reshape(owners, capacity, feat + hd), 'owner', spl...  3.51 us
  transfers between devices with their start and end apart: 6, of which 5 were waited for; matrix products, arithmetic and copies ran while one was open for 0% of the time, Pallas kernels for 10%

profile of v1, /device:TPU:0, one launch (start us, length us, event | category | flops | bytes accessed | tf_op | source)
XLA Modules:
  0.0 82.1 jit_solution(6442765903747863327)
XLA Ops:
  0.0 0.0 copy-start
  0.0 1.9 %route.1 = bf16[64,1024]{1,0:T(8,128)(2,1)} custom-call(s32[1,32]{1,0:T(1,128)} %bitcast.32, s32[1,16]{1,0:T(1,128)} %bitcast.34, bf16[32,1024]{1,0:T(8,128)(2,1)} %q_ref.1), custom_call_target="tpu_custom_call" | custom-call | tf_op jit(solution)/shard_map/route/pallas_call | solution.py:220
  2.0 1.0 %reshape.40 = bf16[16,4,1024]{2,1,0:T(4,128)(2,1)S(1)} reshape(bf16[64,1024]{1,0:T(8,128)(2,1)} %route.1) | data formatting | bytes 262144 | tf_op jit(solution)/shard_map/reshape | solution.py:228
  2.9 15.9 %all_to_all.15 = bf16[16,4,1024]{2,1,0:T(4,128)(2,1)S(1)} all-to-all(bf16[16,4,1024]{2,1,0:T(4,128)(2,1)S(1)} %reshape.40), channel_id=1, replica_groups=mesh['owner'=16,'kv'=8] {'owner'}, dimensions={0} | all-to-all | bytes 262144 | tf_op jit(solution)/shard_map/all_to_all | solution.py:227
  18.8 0.7 reshape.41.x_ref
  19.5 9.4 %prefix.1 = bf16[64,1152]{1,0:T(8,128)(2,1)} custom-call(bf16[64,1024]{1,0:T(8,128)(2,1)} %reshape.41.x_ref, bf16[8192,256]{1,0:T(8,128)(2,1)} %bitcast.36), custom_call_target="tpu_custom_call" | custom-call | flops 2147483648 | bytes 4194304 | tf_op jit(solution)/shard_map/prefix/pallas_call | solution.py:257
  28.9 1.6 %reshape.43 = bf16[16,4,1152]{2,1,0:T(4,128)(2,1)} reshape(bf16[64,1152]{1,0:T(8,128)(2,1)} %prefix.1) | data formatting | bytes 294912 | tf_op jit(solution)/shard_map/reshape | solution.py:279
  30.5 3.5 %all-to-all-start.1 = ((bf16[16,4,1152]{2,1,0:T(4,128)(2,1)}), bf16[16,4,1152]{2,1,0:T(4,128)(2,1)S(1)}, u32[]{:S(2)}, u32[]{:S(2)}) async-start(bf16[16,4,1152]{2,1,0:T(4,128)(2,1)} %reshape.43), calls=%async_computation.1 | async-start | bytes 294912 | tf_op jit(solution)/shard_map/all_to_all | solution.py:278
  34.1 8.6 %suffix.1 = (f32[32,1024]{1,0:T(8,128)}, f32[256,128]{1,0:T(8,128)}) custom-call(s32[32]{0:T(128)} %len_ref.1, bf16[32,1024]{1,0:T(8,128)(2,1)} %q_ref.1, bf16[32,1024,256]{2,1,0:T(8,128)(2,1)} %bitcast.26), custom_call_target="tpu_custom_call" | custom-call | flops 134217728 | bytes 16777216 | tf_op jit(solution)/shard_map/suffix/pallas_call | solution.py:232
  42.6 0.0 all-to-all-done.1
  42.6 0.7 reshape.44.recv_ref
  43.3 2.9 %combine.1 = bf16[16,32,1024]{2,1,0:T(8,128)(2,1)} custom-call(s32[1,32]{1,0:T(1,128)} %bitcast.33, s32[1,16]{1,0:T(1,128)} %bitcast.35, bf16[64,1152]{1,0:T(8,128)(2,1)} %reshape.44.recv_ref, f32[32,1024]{1,0:T(8,128)} %get-tuple-element.7.osuf_ref, f32[256,128]{1,0:T(8,128)} %get-tuple-element.8.lsuf_ref), custom_call_target="tpu_custom_call" | custom-call | tf_op jit(solution)/shard_map/combine/pallas_call | solution.py:286
  46.2 7.2 %all-to-all-start.2 = ((bf16[16,32,1024]{2,1,0:T(8,128)(2,1)}), bf16[16,32,1024]{2,1,0:T(8,128)(2,1)S(1)}, u32[]{:S(2)}, u32[]{:S(2)}) async-start(bf16[16,32,1024]{2,1,0:T(8,128)(2,1)} %combine.1), calls=%async_computation.2 | async-start | bytes 2097152 | tf_op jit(solution)/shard_map/all_to_all | solution.py:293
  53.4 15.8 %all-to-all-done.2 = bf16[16,32,1024]{2,1,0:T(8,128)(2,1)S(1)} async-done(((bf16[16,32,1024]{2,1,0:T(8,128)(2,1)}), bf16[16,32,1024]{2,1,0:T(8,128)(2,1)S(1)}, u32[]{:S(2)}, u32[]{:S(2)}) %all-to-all-start.2) | async-done | bytes 1048608 | tf_op jit(solution)/shard_map/all_to_all | solution.py:293
  69.2 0.1 constant_dynamic-slice_fusion
  69.3 0.0 copy-done
  69.3 0.4 convolution_convert_fusion
  69.7 0.1 collective-permute-start
  69.9 1.4 %collective-permute-done = bf16[256,512]{1,0:T(8,128)(2,1)S(1)} collective-permute-done((bf16[256,512]{1,0:T(8,128)(2,1)S(1)}, bf16[256,512]{1,0:T(8,128)(2,1)S(1)}, u32[]{:S(2)}, u32[]{:S(2)}) %collective-permute-start) | collective-permute-done | bytes 262176 | tf_op jit(solution)/shard_map/ppermute | solution.py:307
  71.3 0.4 convert_add_fusion
  71.9 2.8 %collective-permute-start.3 = (bf16[64,512]{1,0:T(8,128)(2,1)S(1)}, bf16[64,512]{1,0:T(8,128)(2,1)S(1)}, u32[]{:S(2)}, u32[]{:S(2)}) collective-permute-start(bf16[64,512]{1,0:T(8,128)(2,1)S(1)} %get-tuple-element.12), channel_id=1, source_target_pairs={{0,6},{1,7},{2,0},{3,1},{4,2},{5,3},{6,4},{7,5},{8,14},{9,15},{10,... | collective-permute-start | bytes 196616 | tf_op jit(solution)/shard_map/ppermute | solution.py:318
  74.7 0.8 collective-permute-start.2
  75.5 0.9 %collective-permute-start.1 = (bf16[64,512]{1,0:T(8,128)(2,1)S(1)}, bf16[64,512]{1,0:T(8,128)(2,1)S(1)}, u32[]{:S(2)}, u32[]{:S(2)}) collective-permute-start(bf16[64,512]{1,0:T(8,128)(2,1)S(1)} %get-tuple-element.11), channel_id=1, source_target_pairs={{0,2},{1,3},{2,4},{3,5},{4,6},{5,7},{6,0},{7,1},{8,10},{9,11},{10,... | collective-permute-start | bytes 196616 | tf_op jit(solution)/shard_map/ppermute | solution.py:318
  76.4 1.5 %collective-permute-done.3 = bf16[64,512]{1,0:T(8,128)(2,1)S(1)} collective-permute-done((bf16[64,512]{1,0:T(8,128)(2,1)S(1)}, bf16[64,512]{1,0:T(8,128)(2,1)S(1)}, u32[]{:S(2)}, u32[]{:S(2)}) %collective-permute-start.3) | collective-permute-done | bytes 65568 | tf_op jit(solution)/shard_map/ppermute | solution.py:318
  77.9 2.9 %collective-permute-done.2 = bf16[64,512]{1,0:T(8,128)(2,1)S(1)} collective-permute-done((bf16[64,512]{1,0:T(8,128)(2,1)S(1)}, bf16[64,512]{1,0:T(8,128)(2,1)S(1)}, u32[]{:S(2)}, u32[]{:S(2)}) %collective-permute-start.2) | collective-permute-done | bytes 65568 | tf_op jit(solution)/shard_map/ppermute | solution.py:318
  80.8 0.7 collective-permute-done.1
  81.5 0.7 fusion.2
  (2 shorter events, 0.1 us)
Async XLA Ops:
  0.0 69.3 %copy-start = (bf16[1024,512]{1,0:T(8,128)(2,1)S(1)}, bf16[1024,512]{1,0:T(8,128)(2,1)}, u32[]{:S(2)}) copy-start(bf16[1024,512]{1,0:T(8,128)(2,1)} %param.13) | copy-start | bytes 3145732
  30.5 12.1 %all-to-all-start.1 = ((bf16[16,4,1152]{2,1,0:T(4,128)(2,1)}), bf16[16,4,1152]{2,1,0:T(4,128)(2,1)S(1)}, u32[]{:S(2)}, u32[]{:S(2)}) async-start(bf16[16,4,1152]{2,1,0:T(4,128)(2,1)} %reshape.43), calls=%async_computation.1 | async-start | bytes 294912 | tf_op jit(solution)/shard_map/all_to_all | solution.py:278
  46.2 23.0 %all-to-all-start.2 = ((bf16[16,32,1024]{2,1,0:T(8,128)(2,1)}), bf16[16,32,1024]{2,1,0:T(8,128)(2,1)S(1)}, u32[]{:S(2)}, u32[]{:S(2)}) async-start(bf16[16,32,1024]{2,1,0:T(8,128)(2,1)} %combine.1), calls=%async_computation.2 | async-start | bytes 2097152 | tf_op jit(solution)/shard_map/all_to_all | solution.py:293
  69.7 1.6 %collective-permute-start = (bf16[256,512]{1,0:T(8,128)(2,1)S(1)}, bf16[256,512]{1,0:T(8,128)(2,1)S(1)}, u32[]{:S(2)}, u32[]{:S(2)}) collective-permute-start(bf16[256,512]{1,0:T(8,128)(2,1)S(1)} %convolution_convert_fusion), channel_id=1, source_target_pairs={{0,1},{1,0},{2,3},{3,2},{4,5},{5,4},{6,7},{7,6},{8,9},{9,8},{10,11... | collective-permute-start | bytes 786440 | tf_op jit(solution)/shard_map/ppermute | solution.py:307
  71.9 6.0 %collective-permute-start.3 = (bf16[64,512]{1,0:T(8,128)(2,1)S(1)}, bf16[64,512]{1,0:T(8,128)(2,1)S(1)}, u32[]{:S(2)}, u32[]{:S(2)}) collective-permute-start(bf16[64,512]{1,0:T(8,128)(2,1)S(1)} %get-tuple-element.12), channel_id=1, source_target_pairs={{0,6},{1,7},{2,0},{3,1},{4,2},{5,3},{6,4},{7,5},{8,14},{9,15},{10,... | collective-permute-start | bytes 196616 | tf_op jit(solution)/shard_map/ppermute | solution.py:318
  74.7 6.1 %collective-permute-start.2 = (bf16[64,512]{1,0:T(8,128)(2,1)S(1)}, bf16[64,512]{1,0:T(8,128)(2,1)S(1)}, u32[]{:S(2)}, u32[]{:S(2)}) collective-permute-start(bf16[64,512]{1,0:T(8,128)(2,1)S(1)} %get-tuple-element.13), channel_id=1, source_target_pairs={{0,4},{1,5},{2,6},{3,7},{4,0},{5,1},{6,2},{7,3},{8,12},{9,13},{10,... | collective-permute-start | bytes 196616 | tf_op jit(solution)/shard_map/ppermute | solution.py:318
  75.5 6.0 %collective-permute-start.1 = (bf16[64,512]{1,0:T(8,128)(2,1)S(1)}, bf16[64,512]{1,0:T(8,128)(2,1)S(1)}, u32[]{:S(2)}, u32[]{:S(2)}) collective-permute-start(bf16[64,512]{1,0:T(8,128)(2,1)S(1)} %get-tuple-element.11), channel_id=1, source_target_pairs={{0,2},{1,3},{2,4},{3,5},{4,6},{5,7},{6,0},{7,1},{8,10},{9,11},{10,... | collective-permute-start | bytes 196616 | tf_op jit(solution)/shard_map/ppermute | solution.py:318

commit v2 on v1

v2 whole, which is shorter than its diff:
```python
import functools

import jax
import jax.numpy as jnp
from jax import lax
from jax.experimental import pallas as pl
from jax.experimental.pallas import tpu as pltpu
from jax.sharding import PartitionSpec as P

LOG2E = 1.4426950408889634
NT = (((1,), (1,)), ((), ()))
VMEM = pl.BlockSpec(memory_space=pltpu.VMEM)
SMEM = pl.BlockSpec(memory_space=pltpu.SMEM)
ANY = pl.BlockSpec(memory_space=pl.ANY)
MIB = 2**20
GROUP_ROWS = 4


def one_hot_slots(fork_ref, slot_ref, capacity):
    rows = fork_ref.shape[1]
    prefixes = slot_ref.shape[1]
    sub = lax.broadcasted_iota(jnp.int32, (rows, rows), 0)
    lane = lax.broadcasted_iota(jnp.int32, (rows, rows), 1)
    eye = sub == lane
    fork_row = jnp.broadcast_to(fork_ref[...], (rows, rows))
    fork_col = jnp.sum(jnp.where(eye, fork_row, 0), axis=1, keepdims=True)
    picked = fork_col == lax.broadcasted_iota(jnp.int32, (rows, prefixes), 1)
    slots_all = jnp.broadcast_to(slot_ref[...], (rows, prefixes))
    stored_col = jnp.sum(jnp.where(picked, slots_all, 0), axis=1, keepdims=True)
    stored_row = jnp.sum(
        jnp.where(eye, jnp.broadcast_to(stored_col, (rows, rows)), 0), axis=0, keepdims=True
    )
    earlier = (stored_col == stored_row) & (sub < lane)
    rank_row = jnp.sum(earlier.astype(jnp.int32), axis=0, keepdims=True)
    return stored_row, rank_row, prefixes


def half_slots(placed, capacity):
    stored_row, rank_row, prefixes = placed
    rows = stored_row.shape[1]
    place = lax.broadcasted_iota(jnp.int32, (prefixes * 2 * capacity, rows), 0)
    return [
        (place == (stored_row * 2 + half) * capacity + rank_row).astype(jnp.float32)
        for half in range(2)
    ]


def route_kernel(fork_ref, slot_ref, query_ref, out_ref, *, capacity):
    rows, feat = query_ref.shape
    hot = half_slots(one_hot_slots(fork_ref, slot_ref, capacity), capacity)
    for half in range(2):
        cols = slice(half * feat // 2, (half + 1) * feat // 2)
        part = jnp.dot(
            hot[half].astype(jnp.bfloat16), query_ref[:, cols], preferred_element_type=jnp.float32
        )
        if half == 0:
            total = part
        else:
            total = total + part
    out_ref[...] = total.astype(jnp.bfloat16)


def suffix_kernel(
    len_ref, q_ref, kv_hbm, out_ref, lse_ref, kv, sems, q_s, o_s, *, first, group, scale
):
    rows, keys, width = kv.shape
    hd = width // 2
    heads = q_ref.shape[1] // hd
    c2 = scale * LOG2E

    def copy_of(r):
        return pltpu.make_async_copy(kv_hbm.at[first + r], kv.at[r], sems.at[r])

    def issue(r, carry):
        copy_of(r).start()
        return carry

    lax.fori_loop(0, rows, issue, 0)
    for h in range(heads):
        q_s[pl.ds(h, rows, stride=heads), :] = q_ref[
            first : first + rows, h * hd : (h + 1) * hd
        ].astype(jnp.float32)
    span = group * heads

    def step(g, carry):
        def wait(i, c):
            copy_of(g * group + i).wait()
            return c

        lax.fori_loop(0, group, wait, 0)
        row_id = lax.broadcasted_iota(jnp.int32, (span, 1), 0) // heads
        length = jnp.zeros((span, 1), jnp.int32)
        for i in range(group):
            length = jnp.where(row_id == i, len_ref[first + g * group + i], length)
        base = pl.multiple_of(g * span, span)
        s = jnp.concatenate(
            [
                lax.dot_general(
                    q_s[pl.ds(base + i * heads, heads), :].astype(jnp.bfloat16),
                    kv[g * group + i, :, :hd],
                    NT,
                    preferred_element_type=jnp.float32,
                )
                for i in range(group)
            ],
            axis=0,
        )
        live = lax.broadcasted_iota(jnp.int32, (span, keys), 1) < length
        s = jnp.where(live, s, -1e30)
        m = jnp.max(s, axis=-1, keepdims=True)
        p = jnp.where(live, jnp.exp2((s - m) * c2), 0.0)
        total = jnp.sum(p, axis=-1, keepdims=True)
        o = jnp.concatenate(
            [
                jnp.dot(
                    p[i * heads : (i + 1) * heads].astype(jnp.bfloat16),
                    kv[g * group + i, :, hd:],
                    preferred_element_type=jnp.float32,
                )
                for i in range(group)
            ],
            axis=0,
        )
        o_s[pl.ds(base, span), :] = o / total
        lse_ref[pl.ds(base, span), :] = jnp.broadcast_to(m * c2 + jnp.log2(total), (span, hd))
        return carry

    lax.fori_loop(0, rows // group, step, 0)
    for h in range(heads):
        out_ref[:, h * hd : (h + 1) * hd] = o_s[pl.ds(h, rows, stride=heads), :]


def prefix_kernel(
    x_ref, kv, after_ref, out_ref, q_s, s_s, acc_s, vt_s, *, kb, ct, sub, scale
):
    keys = kv.shape[0]
    hd = kv.shape[1] // 2
    slots, feat = x_ref.shape
    heads = feat // hd
    count = slots * heads
    c2 = scale * LOG2E
    qf = jnp.concatenate([x_ref[:, h * hd : (h + 1) * hd] for h in range(heads)], axis=0)
    qf = qf.astype(jnp.float32).T * c2
    hi = qf.astype(jnp.bfloat16)
    q_s[:hd, :] = hi
    q_s[hd:, :] = (qf - hi.astype(jnp.float32)).astype(jnp.bfloat16)
    vt_s[:, hd:, :] = jnp.ones((2, vt_s.shape[1] - hd, kb), jnp.bfloat16)
    tiles = count // ct
    steps = kb // sub
    items = [(c, t) for c in range(keys // kb) for t in range(tiles)]

    def scores(idx, j, highest):
        c, t = items[idx]
        here = slice(c * kb + j * sub, c * kb + (j + 1) * sub)
        k = kv[here, :hd]
        s = jnp.dot(
            jnp.concatenate([k, k], axis=1),
            q_s[:, t * ct : (t + 1) * ct],
            preferred_element_type=jnp.float32,
        )
        s_s[idx % 2, j * sub : (j + 1) * sub, :] = s
        if t == 0:
            vt_s[c % 2, :hd, j * sub : (j + 1) * sub] = kv[here, hd:].T
        top = jnp.max(s.reshape(sub // 8, 8, ct), axis=0)
        return top if highest is None else jnp.maximum(highest, top)

    highest = None
    for j in range(steps):
        highest = scores(0, j, highest)
    m_old = {}
    for idx, (c, t) in enumerate(items):
        cols = slice(t * ct, (t + 1) * ct)
        m = jnp.max(highest, axis=0, keepdims=True)
        if c > 0:
            m = jnp.maximum(m, m_old[t])
        highest, o = None, None
        for j in range(steps):
            if idx + 1 < len(items):
                highest = scores(idx + 1, j, highest)
            here = slice(j * sub, (j + 1) * sub)
            p = jnp.exp2(s_s[idx % 2, here, :] - m).astype(jnp.bfloat16)
            part = jnp.dot(vt_s[c % 2, :, here], p, preferred_element_type=jnp.float32)
            o = part if o is None else o + part
        if c > 0:
            o = o + jnp.exp2(m_old[t] - m) * acc_s[:, cols]
        acc_s[:, cols] = o
        m_old[t] = m
    total = acc_s[hd : hd + 1, :]
    out = (acc_s[:hd, :] / total).T.astype(jnp.bfloat16)
    m_all = jnp.concatenate([m_old[t] for t in range(tiles)], axis=1)
    lse = jnp.broadcast_to(m_all + jnp.log2(total), (hd, count)).T
    lane = lax.broadcasted_iota(jnp.int32, (slots, hd), 1)
    pieces = jnp.zeros((slots, hd), jnp.float32)
    for h in range(heads):
        out_ref[:, h * hd : (h + 1) * hd] = out[h * slots : (h + 1) * slots, :]
        rest = lse[h * slots : (h + 1) * slots, :]
        for j in range(3):
            part = rest.astype(jnp.bfloat16).astype(jnp.float32)
            rest = rest - part
            pieces = jnp.where(lane == j * heads + h, part, pieces)
    out_ref[:, feat:] = pieces.astype(jnp.bfloat16)


def combine_kernel(fork_ref, slot_ref, recv_ref, *refs, capacity, heads):
    out_ref = refs[-1]
    parts = [refs[i : i + 2] for i in range(0, len(refs) - 1, 2)]
    copies, rows, feat = out_ref.shape
    hd = feat // heads
    some = rows // len(parts)
    hot = half_slots(one_hot_slots(fork_ref, slot_ref, capacity), capacity)
    for half in range(2):
        got = jnp.dot(
            hot[half].T.astype(jnp.bfloat16), recv_ref[...], preferred_element_type=jnp.float32
        )
        for i in range(heads // 2):
            h = half * (heads // 2) + i
            cols = slice(h * hd, (h + 1) * hd)
            lse_pre = sum(
                got[:, feat // 2 + j * heads // 2 + i : feat // 2 + j * heads // 2 + i + 1]
                for j in range(3)
            )
            lse_pre = jnp.broadcast_to(lse_pre, (rows, hd))
            lse_suf = jnp.concatenate(
                [ref[pl.ds(h, some, stride=heads), :] for _, ref in parts], axis=0
            )
            o_suf = jnp.concatenate([ref[:, cols] for ref, _ in parts], axis=0)
            top = jnp.maximum(lse_pre, lse_suf)
            a = jnp.exp2(lse_pre - top)
            b = jnp.exp2(lse_suf - top)
            value = (a * got[:, i * hd : (i + 1) * hd] + b * o_suf) / (a + b)
            value = value.astype(jnp.bfloat16)
            for copy in range(copies):
                out_ref[copy, :, cols] = value


def body(queries, prefix_cache, suffix_cache, suffix_len, fork_prefix, prefix_slot, out_weight):
    rows, feat = queries.shape
    keys = prefix_cache.shape[1]
    hd = prefix_cache.shape[3] // 2
    heads = feat // hd
    owners = lax.axis_size("owner")
    prefixes = prefix_slot.shape[0]
    capacity = max(2, 2 * rows // prefixes)
    slots = prefixes * capacity
    scale = hd**-0.5
    fork_row = fork_prefix.reshape(1, rows)
    slot_row = prefix_slot.reshape(1, prefixes)

    def limit(mib):
        return pltpu.CompilerParams(vmem_limit_bytes=mib * MIB)

    places = slots * 2
    outgoing = pl.pallas_call(
        functools.partial(route_kernel, capacity=capacity),
        out_shape=jax.ShapeDtypeStruct((places, feat // 2), jnp.bfloat16),
        in_specs=[VMEM, VMEM, VMEM],
        out_specs=VMEM,
        name="route",
    )(fork_row, slot_row, queries)
    received = lax.all_to_all(
        outgoing.reshape(owners, places // owners, feat // 2),
        "owner",
        split_axis=0,
        concat_axis=0,
        tiled=True,
    )

    suffix_keys = suffix_cache.shape[1]
    some = rows // 2

    def suffix(first):
        return pl.pallas_call(
            functools.partial(suffix_kernel, first=first, group=GROUP_ROWS, scale=scale),
            out_shape=(
                jax.ShapeDtypeStruct((some, feat), jnp.float32),
                jax.ShapeDtypeStruct((some * heads, hd), jnp.float32),
            ),
            in_specs=[SMEM, VMEM, ANY],
            out_specs=(VMEM, VMEM),
            scratch_shapes=[
                pltpu.VMEM((some, suffix_keys, 2 * hd), jnp.bfloat16),
                pltpu.SemaphoreType.DMA((some,)),
                pltpu.VMEM((some * heads, hd), jnp.float32),
                pltpu.VMEM((some * heads, hd), jnp.float32),
            ],
            compiler_params=limit(44),
            cost_estimate=pl.CostEstimate(
                flops=4 * some * heads * suffix_keys * hd,
                bytes_accessed=some * suffix_keys * 4 * hd,
                transcendentals=some * heads * suffix_keys,
            ),
            name="suffix",
        )(suffix_len, queries, suffix_cache.reshape(rows, suffix_keys, 2 * hd))

    suffix_one = suffix(0)

    kb, ct, sub = 2048, 256, 512
    count = slots * heads
    partial = pl.pallas_call(
        functools.partial(prefix_kernel, kb=kb, ct=ct, sub=sub, scale=scale),
        out_shape=jax.ShapeDtypeStruct((places, feat // 2 + hd), jnp.bfloat16),
        in_specs=[VMEM, VMEM, ANY],
        out_specs=VMEM,
        scratch_shapes=[
            pltpu.VMEM((2 * hd, count), jnp.bfloat16),
            pltpu.VMEM((2, kb, ct), jnp.float32),
            pltpu.VMEM((hd + 16, count), jnp.float32),
            pltpu.VMEM((2, hd + 16, kb), jnp.bfloat16),
        ],
        compiler_params=limit(24),
        cost_estimate=pl.CostEstimate(
            flops=4 * count * keys * hd,
            bytes_accessed=keys * 4 * hd,
            transcendentals=count * keys,
        ),
        name="prefix",
    )(
        received.reshape(places, feat // 2),
        prefix_cache.reshape(keys, 2 * hd),
        suffix_one[1],
    )
    returned = lax.all_to_all(
        partial.reshape(owners, places // owners, feat // 2 + hd),
        "owner",
        split_axis=0,
        concat_axis=0,
        tiled=True,
    )
    suffix_two = suffix(some)

    attended = pl.pallas_call(
        functools.partial(combine_kernel, capacity=capacity, heads=heads),
        out_shape=jax.ShapeDtypeStruct((owners, rows, feat), jnp.bfloat16),
        in_specs=[VMEM] * 7,
        out_specs=VMEM,
        compiler_params=limit(8),
        name="combine",
    )(fork_row, slot_row, returned.reshape(places, feat // 2 + hd), *suffix_one, *suffix_two)
    gathered = lax.all_to_all(attended, "owner", split_axis=0, concat_axis=0, tiled=True)

    members = lax.axis_size("kv")
    chips = members // 2
    place = lax.axis_index("kv")
    chip, core = place // 2, place % 2
    block = owners * rows // members
    cols = out_weight.shape[1]
    full = gathered.reshape(chips, 2, block, feat)
    theirs = jnp.dot(
        lax.dynamic_index_in_dim(full, 1 - core, 1, keepdims=False).reshape(chips * block, feat),
        out_weight,
        preferred_element_type=jnp.float32,
    ).astype(jnp.bfloat16)
    from_pair = lax.ppermute(theirs, "kv", [(i, i ^ 1) for i in range(members)])
    mine = jnp.dot(
        lax.dynamic_index_in_dim(full, core, 1, keepdims=False).reshape(chips * block, feat),
        out_weight,
        preferred_element_type=jnp.float32,
    )
    pair_sum = (mine + from_pair.astype(jnp.float32)).reshape(chips, block, cols)
    pair_sent = pair_sum.astype(jnp.bfloat16)
    total = lax.dynamic_index_in_dim(pair_sum, chip, 0, keepdims=False)
    for d in range(1, chips):
        piece = lax.dynamic_index_in_dim(pair_sent, (chip + d) % chips, 0, keepdims=False)
        moved = lax.ppermute(
            piece,
            "kv",
            [(x * 2 + c, ((x + d) % chips) * 2 + c) for x in range(chips) for c in range(2)],
        )
        total = total + moved.astype(jnp.float32)
    return total.astype(jnp.bfloat16)


def solution(mesh):
    placed = (
        P("owner", "kv"),
        P("owner", None, "kv", None),
        P("owner", None, "kv", None),
        P("owner"),
        P("owner", None),
        P(),
        P("kv", "owner"),
    )
    return jax.shard_map(
        body, mesh=mesh, in_specs=placed, out_specs=P("kv", "owner"), check_vma=False
    )
```

time: 82.6 us -> 75.8 us (0.918)
  blocking collectives: 15.9 us -> 0 us
  starting transfers between devices: 15.3 us -> 22.1 us
  waiting for transfers between devices: 22.4 us -> 28 us
  Pallas kernels: 22.8 us -> 19.7 us
    all_to_all x1 -> x0, blocking collectives: 15.9 us -> none  [body(): lax.all_to_all(outgoing.reshape(owners, capacity, feat), 'owner', split_a...]
    all_to_all x1 -> x2, starting transfers between devices: 3.51 us -> 13.6 us  [the longest x1 8.13 us: body(): lax.all_to_all(outgoing.reshape(owners, places // owners, feat // 2), 'ow...]
    all_to_all x1 -> x2, waiting for transfers between devices: 0.01 us -> 5.15 us  [the longest x1 3.41 us: body(): lax.all_to_all(partial.reshape(owners, places // owners, feat // 2 + hd),...]
    reshape x4 -> x0, local copies, waits for them, and re-layouts: 3.92 us -> none  [the longest x1 1.6 us: body(): partial.reshape(owners, capacity, feat + hd)]
    unnamed x2 -> x16, local copies, waits for them, and re-layouts: 0.01 us -> 3.7 us
    all_to_all x1, starting transfers between devices: 7.15 us -> 3.83 us  [body(): lax.all_to_all(attended, 'owner', split_axis=0, concat_axis=0, tiled=True)]
    pallas_call x2 -> x3, Pallas kernels: 18 us -> 15.9 us  [the longest x2 9.44 us: suffix(): pl.pallas_call(functools.partial(suffix_kernel, first=first, group=GROUP_...]
    pallas_call x1, Pallas kernels: 2.86 us -> 1.77 us  [body(): pl.pallas_call(functools.partial(combine_kernel, capacity=capacity, heads...]
  transfers between devices with their start and end apart: 6 -> 7, of which waited for: 5 -> 7; matrix products, arithmetic and copies ran while one was open for 0% -> 0% of each run, Pallas kernels for 10% -> 13%
where the time goes in v2:
time: 75.8 us; the launch traced here: 75.3 us
  waiting for transfers between devices  28 us (37%)
  starting transfers between devices  22.1 us (29%)
  Pallas kernels  19.7 us (26%)
  local copies, waits for them, and re-layouts  3.79 us (5%)
  matrix products  0.87 us (1%)
    all_to_all x1, waiting for transfers between devices, body(): lax.all_to_all(attended, 'owner', split_axis=0, concat_axis=0, tiled=True)  16.3 us
    pallas_call x2, Pallas kernels, suffix(): pl.pallas_call(functools.partial(suffix_kernel, first=first, group=GROUP_...  9.44 us
    all_to_all x1, starting transfers between devices, body(): lax.all_to_all(outgoing.reshape(owners, places // owners, feat // 2), 'ow...  8.13 us
    pallas_call x1, Pallas kernels, body(): pl.pallas_call(functools.partial(prefix_kernel, kb=kb, ct=ct, sub=sub, sc...  6.49 us
    all_to_all x1, starting transfers between devices, body(): lax.all_to_all(partial.reshape(owners, places // owners, feat // 2 + hd),...  5.48 us
    ppermute x3, waiting for transfers between devices, body(): lax.ppermute(piece, 'kv', [(x * 2 + c, (x + d) % chips * 2 + c) for x in...  5.07 us
    ppermute x3, starting transfers between devices, body(): lax.ppermute(piece, 'kv', [(x * 2 + c, (x + d) % chips * 2 + c) for x in...  4.53 us
    all_to_all x1, starting transfers between devices, body(): lax.all_to_all(attended, 'owner', split_axis=0, concat_axis=0, tiled=True)  3.83 us
  transfers between devices with their start and end apart: 7, of which 7 were waited for; matrix products, arithmetic and copies ran while one was open for 0% of the time, Pallas kernels for 13%

profile of v2, /device:TPU:0, one launch (start us, length us, event | category | flops | bytes accessed | tf_op | source)
XLA Modules:
  0.0 75.3 jit_solution(13111321440195662261)
XLA Ops:
  0.0 0.0 copy-start
  0.0 0.0 copy-start.2
  0.0 0.0 copy-start.4
  0.0 2.0 %route.1 = bf16[128,512]{1,0:T(8,128)(2,1)} custom-call(s32[1,32]{1,0:T(1,128)} %bitcast.32, s32[1,16]{1,0:T(1,128)} %bitcast.34, bf16[32,1024]{1,0:T(8,128)(2,1)} %q_ref.3), custom_call_target="tpu_custom_call" | custom-call | tf_op jit(solution)/shard_map/route/pallas_call | solution.py:253
  2.0 8.1 %all-to-all-start = ((bf16[16,8,512]{2,1,0:T(8,128)(2,1)}), bf16[16,8,512]{2,1,0:T(8,128)(2,1)S(1)}, u32[]{:S(2)}, u32[]{:S(2)}) async-start(bf16[16,8,512]{2,1,0:T(8,128)(2,1)} %bitcast.44), calls=%async_computation | async-start | bytes 262144 | tf_op jit(solution)/shard_map/all_to_all | solution.py:260
  10.1 0.0 copy-start.1
  10.2 0.8 %copy-done.1 = bf16[32,1024]{1,0:T(8,128)(2,1)S(1)} copy-done((bf16[32,1024]{1,0:T(8,128)(2,1)S(1)}, bf16[32,1024]{1,0:T(8,128)(2,1)}, u32[]{:S(2)}) %copy-start.1) | copy-done | bytes 65560
  11.0 0.0 copy-start.3
  11.0 0.7 copy-done.3
  11.6 4.7 %suffix.2 = (f32[16,1024]{1,0:T(8,128)S(1)}, f32[128,128]{1,0:T(8,128)S(1)}) custom-call(s32[32]{0:T(128)S(1)} %copy-done.3, bf16[32,1024]{1,0:T(8,128)(2,1)S(1)} %copy-done.1, bf16[32,1024,256]{2,1,0:T(8,128)(2,1)} %bitcast.37), custom_call_target="tpu_custom_call" | custom-call | flops 67108864 | bytes 8388608 | tf_op jit(solution)/shard_map/suffix/pallas_call | solution.py:272
  16.4 0.0 copy-start.5
  16.4 0.0 copy-start.6
  16.4 1.7 %all-to-all-done = bf16[16,8,512]{2,1,0:T(8,128)(2,1)S(1)} async-done(((bf16[16,8,512]{2,1,0:T(8,128)(2,1)}), bf16[16,8,512]{2,1,0:T(8,128)(2,1)S(1)}, u32[]{:S(2)}, u32[]{:S(2)}) %all-to-all-start) | async-done | bytes 131104 | tf_op jit(solution)/shard_map/all_to_all | solution.py:260
  18.1 0.0 copy-start.7
  18.1 2.2 %copy-done.7 = bf16[1,8192,1,256]{3,1,2,0:T(8,128)(2,1)S(1)} copy-done((bf16[1,8192,1,256]{3,1,2,0:T(8,128)(2,1)S(1)}, bf16[1,8192,1,256]{3,1,2,0:T(8,128)(2,1)}, u32[]{:S(2)}) %copy-start.7) | copy-done | bytes 4194328
  20.3 6.5 %prefix.1 = bf16[128,640]{1,0:T(8,128)(2,1)} custom-call(bf16[128,512]{1,0:T(8,128)(2,1)S(1)} %bitcast.31, bf16[8192,256]{1,0:T(8,128)(2,1)S(1)} %bitcast.36, f32[128,128]{1,0:T(8,128)S(1)} %get-tuple-element.9.after_ref.refs_1_), custom_call_target="tpu_custom_call" | custom-call | flops 2147483648 | bytes 4194304 | tf_op jit(solution)/shard_map/prefix/pallas_call | solution.py:299
  26.8 5.5 %all-to-all-start.1 = ((bf16[16,8,640]{2,1,0:T(8,128)(2,1)}), bf16[16,8,640]{2,1,0:T(8,128)(2,1)S(1)}, u32[]{:S(2)}, u32[]{:S(2)}) async-start(bf16[16,8,640]{2,1,0:T(8,128)(2,1)} %bitcast.6), calls=%async_computation.1 | async-start | bytes 327680 | tf_op jit(solution)/shard_map/all_to_all | solution.py:322
  32.3 0.0 copy-done.2
  32.3 0.0 copy-done.4
  32.3 4.7 %suffix.3 = (f32[16,1024]{1,0:T(8,128)S(1)}, f32[128,128]{1,0:T(8,128)S(1)}) custom-call(s32[32]{0:T(128)S(1)} %copy-done.4, bf16[32,1024]{1,0:T(8,128)(2,1)S(1)} %copy-done.2, bf16[32,1024,256]{2,1,0:T(8,128)(2,1)} %bitcast.38), custom_call_target="tpu_custom_call" | custom-call | flops 67108864 | bytes 8388608 | tf_op jit(solution)/shard_map/suffix/pallas_call | solution.py:272
  37.1 3.4 %all-to-all-done.1 = bf16[16,8,640]{2,1,0:T(8,128)(2,1)S(1)} async-done(((bf16[16,8,640]{2,1,0:T(8,128)(2,1)}), bf16[16,8,640]{2,1,0:T(8,128)(2,1)S(1)}, u32[]{:S(2)}, u32[]{:S(2)}) %all-to-all-start.1) | async-done | bytes 163872 | tf_op jit(solution)/shard_map/all_to_all | solution.py:322
  40.5 0.0 copy-done.5
  40.5 0.0 copy-done.6
  40.5 1.8 %combine.1 = bf16[16,32,1024]{2,1,0:T(8,128)(2,1)} custom-call(s32[1,32]{1,0:T(1,128)S(1)} %bitcast.33, s32[1,16]{1,0:T(1,128)S(1)} %bitcast.35, bf16[128,640]{1,0:T(8,128)(2,1)S(1)} %bitcast.30, f32[16,1024]{1,0:T(8,128)S(1)} %get-tuple-element.10.refs_0_, f32[128,128]{1,0:T(8,128)S(1)} %get-tuple-element.9.after_ref.refs_1_, ...), custom_call_target="tpu_custom_call" | custom-call | tf_op jit(solution)/shard_map/combine/pallas_call | solution.py:331
  42.3 3.8 %all-to-all-start.2 = ((bf16[16,32,1024]{2,1,0:T(8,128)(2,1)}), bf16[16,32,1024]{2,1,0:T(8,128)(2,1)S(1)}, u32[]{:S(2)}, u32[]{:S(2)}) async-start(bf16[16,32,1024]{2,1,0:T(8,128)(2,1)} %combine.1), calls=%async_computation.2 | async-start | bytes 2097152 | tf_op jit(solution)/shard_map/all_to_all | solution.py:339
  46.1 16.3 %all-to-all-done.2 = bf16[16,32,1024]{2,1,0:T(8,128)(2,1)S(1)} async-done(((bf16[16,32,1024]{2,1,0:T(8,128)(2,1)}), bf16[16,32,1024]{2,1,0:T(8,128)(2,1)S(1)}, u32[]{:S(2)}, u32[]{:S(2)}) %all-to-all-start.2) | async-done | bytes 1048608 | tf_op jit(solution)/shard_map/all_to_all | solution.py:339
  62.4 0.1 constant_dynamic-slice_fusion
  62.5 0.0 copy-done
  62.5 0.4 convolution_convert_fusion
  63.0 0.1 collective-permute-start
  63.1 1.4 %collective-permute-done = bf16[256,512]{1,0:T(8,128)(2,1)S(1)} collective-permute-done((bf16[256,512]{1,0:T(8,128)(2,1)S(1)}, bf16[256,512]{1,0:T(8,128)(2,1)S(1)}, u32[]{:S(2)}, u32[]{:S(2)}) %collective-permute-start) | collective-permute-done | bytes 262176 | tf_op jit(solution)/shard_map/ppermute | solution.py:353
  64.6 0.4 convert_add_fusion
  65.1 2.8 %collective-permute-start.3 = (bf16[64,512]{1,0:T(8,128)(2,1)S(1)}, bf16[64,512]{1,0:T(8,128)(2,1)S(1)}, u32[]{:S(2)}, u32[]{:S(2)}) collective-permute-start(bf16[64,512]{1,0:T(8,128)(2,1)S(1)} %get-tuple-element.16), channel_id=1, source_target_pairs={{0,6},{1,7},{2,0},{3,1},{4,2},{5,3},{6,4},{7,5},{8,14},{9,15},{10,... | collective-permute-start | bytes 196616 | tf_op jit(solution)/shard_map/ppermute | solution.py:364
  67.9 0.8 %collective-permute-start.2 = (bf16[64,512]{1,0:T(8,128)(2,1)S(1)}, bf16[64,512]{1,0:T(8,128)(2,1)S(1)}, u32[]{:S(2)}, u32[]{:S(2)}) collective-permute-start(bf16[64,512]{1,0:T(8,128)(2,1)S(1)} %get-tuple-element.17), channel_id=1, source_target_pairs={{0,4},{1,5},{2,6},{3,7},{4,0},{5,1},{6,2},{7,3},{8,12},{9,13},{10,... | collective-permute-start | bytes 196616 | tf_op jit(solution)/shard_map/ppermute | solution.py:364
  68.7 0.9 %collective-permute-start.1 = (bf16[64,512]{1,0:T(8,128)(2,1)S(1)}, bf16[64,512]{1,0:T(8,128)(2,1)S(1)}, u32[]{:S(2)}, u32[]{:S(2)}) collective-permute-start(bf16[64,512]{1,0:T(8,128)(2,1)S(1)} %get-tuple-element.15), channel_id=1, source_target_pairs={{0,2},{1,3},{2,4},{3,5},{4,6},{5,7},{6,0},{7,1},{8,10},{9,11},{10,... | collective-permute-start | bytes 196616 | tf_op jit(solution)/shard_map/ppermute | solution.py:364
  69.6 1.5 %collective-permute-done.3 = bf16[64,512]{1,0:T(8,128)(2,1)S(1)} collective-permute-done((bf16[64,512]{1,0:T(8,128)(2,1)S(1)}, bf16[64,512]{1,0:T(8,128)(2,1)S(1)}, u32[]{:S(2)}, u32[]{:S(2)}) %collective-permute-start.3) | collective-permute-done | bytes 65568 | tf_op jit(solution)/shard_map/ppermute | solution.py:364
  71.1 2.9 %collective-permute-done.2 = bf16[64,512]{1,0:T(8,128)(2,1)S(1)} collective-permute-done((bf16[64,512]{1,0:T(8,128)(2,1)S(1)}, bf16[64,512]{1,0:T(8,128)(2,1)S(1)}, u32[]{:S(2)}, u32[]{:S(2)}) %collective-permute-start.2) | collective-permute-done | bytes 65568 | tf_op jit(solution)/shard_map/ppermute | solution.py:364
  74.0 0.7 collective-permute-done.1
  74.7 0.7 fusion.2
  (2 shorter events, 0.1 us)
Async XLA Ops:
  0.0 62.5 %copy-start = (bf16[1024,512]{1,0:T(8,128)(2,1)S(1)}, bf16[1024,512]{1,0:T(8,128)(2,1)}, u32[]{:S(2)}) copy-start(bf16[1024,512]{1,0:T(8,128)(2,1)} %param.13) | copy-start | bytes 3145732
  0.0 32.3 %copy-start.2 = (bf16[32,1024]{1,0:T(8,128)(2,1)S(1)}, bf16[32,1024]{1,0:T(8,128)(2,1)}, u32[]{:S(2)}) copy-start(bf16[32,1024]{1,0:T(8,128)(2,1)} %q_ref.3) | copy-start | bytes 196612
  0.0 32.3 %copy-start.4 = (s32[32]{0:T(128)S(1)}, s32[32]{0:T(128)}, u32[]{:S(2)}) copy-start(s32[32]{0:T(128)} %len_ref.3) | copy-start | bytes 388
  2.0 16.1 %all-to-all-start = ((bf16[16,8,512]{2,1,0:T(8,128)(2,1)}), bf16[16,8,512]{2,1,0:T(8,128)(2,1)S(1)}, u32[]{:S(2)}, u32[]{:S(2)}) async-start(bf16[16,8,512]{2,1,0:T(8,128)(2,1)} %bitcast.44), calls=%async_computation | async-start | bytes 262144 | tf_op jit(solution)/shard_map/all_to_all | solution.py:260
  10.1 0.8 %copy-start.1 = (bf16[32,1024]{1,0:T(8,128)(2,1)S(1)}, bf16[32,1024]{1,0:T(8,128)(2,1)}, u32[]{:S(2)}) copy-start(bf16[32,1024]{1,0:T(8,128)(2,1)} %q_ref.3) | copy-start | bytes 196612
  11.0 0.7 copy-start.3
  16.4 24.1 %copy-start.5 = (s32[32,1]{0,1:T(1,128)S(1)}, s32[32,1]{0,1:T(1,128)}, u32[]{:S(2)}) copy-start(s32[32,1]{0,1:T(1,128)} %param.11) | copy-start | bytes 388
  16.4 24.1 %copy-start.6 = (s32[16]{0:T(128)S(1)}, s32[16]{0:T(128)}, u32[]{:S(2)}) copy-start(s32[16]{0:T(128)} %param.12) | copy-start | bytes 196
  18.1 2.2 %copy-start.7 = (bf16[1,8192,1,256]{3,1,2,0:T(8,128)(2,1)S(1)}, bf16[1,8192,1,256]{3,1,2,0:T(8,128)(2,1)}, u32[]{:S(2)}) copy-start(bf16[1,8192,1,256]{3,1,2,0:T(8,128)(2,1)} %param.8) | copy-start | bytes 12582916
  26.8 13.7 %all-to-all-start.1 = ((bf16[16,8,640]{2,1,0:T(8,128)(2,1)}), bf16[16,8,640]{2,1,0:T(8,128)(2,1)S(1)}, u32[]{:S(2)}, u32[]{:S(2)}) async-start(bf16[16,8,640]{2,1,0:T(8,128)(2,1)} %bitcast.6), calls=%async_computation.1 | async-start | bytes 327680 | tf_op jit(solution)/shard_map/all_to_all | solution.py:322
  42.3 20.2 %all-to-all-start.2 = ((bf16[16,32,1024]{2,1,0:T(8,128)(2,1)}), bf16[16,32,1024]{2,1,0:T(8,128)(2,1)S(1)}, u32[]{:S(2)}, u32[]{:S(2)}) async-start(bf16[16,32,1024]{2,1,0:T(8,128)(2,1)} %combine.1), calls=%async_computation.2 | async-start | bytes 2097152 | tf_op jit(solution)/shard_map/all_to_all | solution.py:339
  63.0 1.6 %collective-permute-start = (bf16[256,512]{1,0:T(8,128)(2,1)S(1)}, bf16[256,512]{1,0:T(8,128)(2,1)S(1)}, u32[]{:S(2)}, u32[]{:S(2)}) collective-permute-start(bf16[256,512]{1,0:T(8,128)(2,1)S(1)} %convolution_convert_fusion), channel_id=1, source_target_pairs={{0,1},{1,0},{2,3},{3,2},{4,5},{5,4},{6,7},{7,6},{8,9},{9,8},{10,11... | collective-permute-start | bytes 786440 | tf_op jit(solution)/shard_map/ppermute | solution.py:353
  65.1 6.1 %collective-permute-start.3 = (bf16[64,512]{1,0:T(8,128)(2,1)S(1)}, bf16[64,512]{1,0:T(8,128)(2,1)S(1)}, u32[]{:S(2)}, u32[]{:S(2)}) collective-permute-start(bf16[64,512]{1,0:T(8,128)(2,1)S(1)} %get-tuple-element.16), channel_id=1, source_target_pairs={{0,6},{1,7},{2,0},{3,1},{4,2},{5,3},{6,4},{7,5},{8,14},{9,15},{10,... | collective-permute-start | bytes 196616 | tf_op jit(solution)/shard_map/ppermute | solution.py:364
  67.9 6.1 %collective-permute-start.2 = (bf16[64,512]{1,0:T(8,128)(2,1)S(1)}, bf16[64,512]{1,0:T(8,128)(2,1)S(1)}, u32[]{:S(2)}, u32[]{:S(2)}) collective-permute-start(bf16[64,512]{1,0:T(8,128)(2,1)S(1)} %get-tuple-element.17), channel_id=1, source_target_pairs={{0,4},{1,5},{2,6},{3,7},{4,0},{5,1},{6,2},{7,3},{8,12},{9,13},{10,... | collective-permute-start | bytes 196616 | tf_op jit(solution)/shard_map/ppermute | solution.py:364
  68.7 6.0 %collective-permute-start.1 = (bf16[64,512]{1,0:T(8,128)(2,1)S(1)}, bf16[64,512]{1,0:T(8,128)(2,1)S(1)}, u32[]{:S(2)}, u32[]{:S(2)}) collective-permute-start(bf16[64,512]{1,0:T(8,128)(2,1)S(1)} %get-tuple-element.15), channel_id=1, source_target_pairs={{0,2},{1,3},{2,4},{3,5},{4,6},{5,7},{6,0},{7,1},{8,10},{9,11},{10,... | collective-permute-start | bytes 196616 | tf_op jit(solution)/shard_map/ppermute | solution.py:364

commit v3 on v2

--- a/solution.py
+++ b/solution.py
@@ -16,16 +16,14 @@
 GROUP_ROWS = 4
 
 
-def one_hot_slots(fork_ref, slot_ref, capacity):
-    rows = fork_ref.shape[1]
-    prefixes = slot_ref.shape[1]
+def one_hot_slots(ints_ref, rows, prefixes, capacity):
     sub = lax.broadcasted_iota(jnp.int32, (rows, rows), 0)
     lane = lax.broadcasted_iota(jnp.int32, (rows, rows), 1)
     eye = sub == lane
-    fork_row = jnp.broadcast_to(fork_ref[...], (rows, rows))
+    fork_row = jnp.broadcast_to(ints_ref[:, :rows], (rows, rows))
     fork_col = jnp.sum(jnp.where(eye, fork_row, 0), axis=1, keepdims=True)
     picked = fork_col == lax.broadcasted_iota(jnp.int32, (rows, prefixes), 1)
-    slots_all = jnp.broadcast_to(slot_ref[...], (rows, prefixes))
+    slots_all = jnp.broadcast_to(ints_ref[:, rows : rows + prefixes], (rows, prefixes))
     stored_col = jnp.sum(jnp.where(picked, slots_all, 0), axis=1, keepdims=True)
     stored_row = jnp.sum(
         jnp.where(eye, jnp.broadcast_to(stored_col, (rows, rows)), 0), axis=0, keepdims=True
@@ -45,9 +43,10 @@
     ]
 
 
-def route_kernel(fork_ref, slot_ref, query_ref, out_ref, *, capacity):
+def route_kernel(ints_ref, query_ref, out_ref, query_out, *, prefixes, capacity):
+    query_out[...] = query_ref[...]
     rows, feat = query_ref.shape
-    hot = half_slots(one_hot_slots(fork_ref, slot_ref, capacity), capacity)
+    hot = half_slots(one_hot_slots(ints_ref, rows, prefixes, capacity), capacity)
     for half in range(2):
         cols = slice(half * feat // 2, (half + 1) * feat // 2)
         part = jnp.dot(
@@ -61,54 +60,79 @@
 
 
 def suffix_kernel(
-    len_ref, q_ref, kv_hbm, out_ref, lse_ref, kv, sems, q_s, o_s, *, first, group, scale
+    len_hbm,
+    q_hbm,
+    kv_hbm,
+    out_ref,
+    lse_ref,
+    kv,
+    sems,
+    lens,
+    q,
+    q_s,
+    o_s,
+    sem_l,
+    sem_q,
+    *,
+    first,
+    skip,
+    group,
+    scale,
 ):
     rows, keys, width = kv.shape
     hd = width // 2
-    heads = q_ref.shape[1] // hd
+    heads = q.shape[1] // hd
     c2 = scale * LOG2E
-
-    def copy_of(r):
+    span = group * heads
+    groups = rows // group
+
+    def rows_copy(r):
         return pltpu.make_async_copy(kv_hbm.at[first + r], kv.at[r], sems.at[r])
 
-    def issue(r, carry):
-        copy_of(r).start()
-        return carry
-
-    lax.fori_loop(0, rows, issue, 0)
+    copy_l = pltpu.make_async_copy(len_hbm, lens, sem_l)
+    copy_q = pltpu.make_async_copy(q_hbm, q, sem_q)
+    copy_l.start()
+    copy_q.start()
+    for r in range(rows):
+        rows_copy(r).start()
+    copy_q.wait()
     for h in range(heads):
-        q_s[pl.ds(h, rows, stride=heads), :] = q_ref[
+        q_s[pl.ds(h, rows, stride=heads), :] = q[
             first : first + rows, h * hd : (h + 1) * hd
         ].astype(jnp.float32)
-    span = group * heads
-
-    def step(g, carry):
-        def wait(i, c):
-            copy_of(g * group + i).wait()
-            return c
-
-        lax.fori_loop(0, group, wait, 0)
-        row_id = lax.broadcasted_iota(jnp.int32, (span, 1), 0) // heads
-        length = jnp.zeros((span, 1), jnp.int32)
-        for i in range(group):
-            length = jnp.where(row_id == i, len_ref[first + g * group + i], length)
-        base = pl.multiple_of(g * span, span)
-        s = jnp.concatenate(
+    copy_l.wait()
+    row_id = lax.broadcasted_iota(jnp.int32, (span, 1), 0) // heads
+    position = lax.broadcasted_iota(jnp.int32, (span, keys), 1)
+
+    def scores(g):
+        return jnp.concatenate(
             [
                 lax.dot_general(
-                    q_s[pl.ds(base + i * heads, heads), :].astype(jnp.bfloat16),
-                    kv[g * group + i, :, :hd],
+                    q_s[r * heads : (r + 1) * heads, :].astype(jnp.bfloat16),
+                    kv[r, :, :hd],
                     NT,
                     preferred_element_type=jnp.float32,
                 )
-                for i in range(group)
+                for r in range(g * group, (g + 1) * group)
             ],
             axis=0,
         )
-        live = lax.broadcasted_iota(jnp.int32, (span, keys), 1) < length
-        s = jnp.where(live, s, -1e30)
+
+    for r in range(group):
+        rows_copy(r).wait()
+    s_next = scores(0)
+    for g in range(groups):
+        s = s_next
+        if g + 1 < groups:
+            for r in range((g + 1) * group, (g + 2) * group):
+                rows_copy(r).wait()
+            s_next = scores(g + 1)
+        length = jnp.zeros((span, 1), jnp.int32)
+        for i in range(group):
+            length = jnp.where(row_id == i, lens[0, skip + first + g * group + i], length)
+        s = jnp.where(position < length, s, -1e30)
         m = jnp.max(s, axis=-1, keepdims=True)
-        p = jnp.where(live, jnp.exp2((s - m) * c2), 0.0)
+        p = jnp.exp2((s - m) * c2)
         total = jnp.sum(p, axis=-1, keepdims=True)
         o = jnp.concatenate(
             [
@@ -121,11 +145,10 @@
             ],
             axis=0,
         )
-        o_s[pl.ds(base, span), :] = o / total
-        lse_ref[pl.ds(base, span), :] = jnp.broadcast_to(m * c2 + jnp.log2(total), (span, hd))
-        return carry
-
-    lax.fori_loop(0, rows // group, step, 0)
+        o_s[g * span : (g + 1) * span, :] = o / total
+        lse_ref[g * span : (g + 1) * span, :] = jnp.broadcast_to(
+            m * c2 + jnp.log2(total), (span, hd)
+        )
     for h in range(heads):
         out_ref[:, h * hd : (h + 1) * hd] = o_s[pl.ds(h, rows, stride=heads), :]
 
@@ -201,13 +224,13 @@
     out_ref[:, feat:] = pieces.astype(jnp.bfloat16)
 
 
-def combine_kernel(fork_ref, slot_ref, recv_ref, *refs, capacity, heads):
+def combine_kernel(ints_ref, recv_ref, *refs, prefixes, capacity, heads):
     out_ref = refs[-1]
     parts = [refs[i : i + 2] for i in range(0, len(refs) - 1, 2)]
-    copies, rows, feat = out_ref.shape
+    rows, feat = out_ref.shape
     hd = feat // heads
     some = rows // len(parts)
-    hot = half_slots(one_hot_slots(fork_ref, slot_ref, capacity), capacity)
+    hot = half_slots(one_hot_slots(ints_ref, rows, prefixes, capacity), capacity)
     for half in range(2):
         got = jnp.dot(
             hot[half].T.astype(jnp.bfloat16), recv_ref[...], preferred_element_type=jnp.float32
@@ -228,9 +251,30 @@
             a = jnp.exp2(lse_pre - top)
             b = jnp.exp2(lse_suf - top)
             value = (a * got[:, i * hd : (i + 1) * hd] + b * o_suf) / (a + b)
-            value = value.astype(jnp.bfloat16)
-            for copy in range(copies):
-                out_ref[copy, :, cols] = value
+            out_ref[:, cols] = value.astype(jnp.bfloat16)
+
+
+def project_kernel(rows_ref, weight_ref, out_ref, *, other):
+    chips, block, cols = out_ref.shape
+    core = lax.rem(lax.axis_index("kv") + other, 2)
+    left = jnp.concatenate(
+        [
+            rows_ref[pl.ds(pl.multiple_of((2 * x + core) * block, block), block), :]
+            for x in range(chips)
+        ],
+        axis=0,
+    )
+    total = jnp.dot(left, weight_ref[...], preferred_element_type=jnp.float32)
+    out_ref[...] = total.reshape(chips, block, cols).astype(out_ref.dtype)
+
+
+def pair_kernel(mine_ref, other_ref, total_ref, *piece_refs):
+    chips = mine_ref.shape[0]
+    chip = lax.axis_index("kv") // 2
+    total_ref[...] = mine_ref[chip] + other_ref[chip].astype(jnp.float32)
+    for d, piece_ref in enumerate(piece_refs, 1):
+        x = lax.rem(chip + d, chips)
+        piece_ref[...] = (mine_ref[x] + other_ref[x].astype(jnp.float32)).astype(jnp.bfloat16)
 
 
 def body(queries, prefix_cache, suffix_cache, suffix_len, fork_prefix, prefix_slot, out_weight):
@@ -243,20 +287,23 @@
     capacity = max(2, 2 * rows // prefixes)
     slots = prefixes * capacity
     scale = hd**-0.5
-    fork_row = fork_prefix.reshape(1, rows)
-    slot_row = prefix_slot.reshape(1, prefixes)
+    ints = jnp.concatenate([fork_prefix.reshape(rows), prefix_slot, suffix_len]).reshape(1, -1)
 
     def limit(mib):
         return pltpu.CompilerParams(vmem_limit_bytes=mib * MIB)
 
     places = slots * 2
-    outgoing = pl.pallas_call(
-        functools.partial(route_kernel, capacity=capacity),
-        out_shape=jax.ShapeDtypeStruct((places, feat // 2), jnp.bfloat16),
-        in_specs=[VMEM, VMEM, VMEM],
-        out_specs=VMEM,
+    outgoing, queries_near = pl.pallas_call(
+        functools.partial(route_kernel, prefixes=prefixes, capacity=capacity),
+        out_shape=(
+            jax.ShapeDtypeStruct((places, feat // 2), jnp.bfloat16),
+            jax.ShapeDtypeStruct(queries.shape, queries.dtype),
+        ),
+        in_specs=[VMEM] * 2,
+        out_specs=(VMEM,) * 2,
+        compiler_params=limit(40),
         name="route",
-    )(fork_row, slot_row, queries)
+    )(ints, queries)
     received = lax.all_to_all(
         outgoing.reshape(owners, places // owners, feat // 2),
         "owner",
@@ -268,33 +315,37 @@
     suffix_keys = suffix_cache.shape[1]
     some = rows // 2
 
-    def suffix(first):
+    def suffix(first, room):
         return pl.pallas_call(
-            functools.partial(suffix_kernel, first=first, group=GROUP_ROWS, scale=scale),
+            functools.partial(suffix_kernel, first=first, skip=rows + prefixes, group=GROUP_ROWS, scale=scale),
             out_shape=(
                 jax.ShapeDtypeStruct((some, feat), jnp.float32),
                 jax.ShapeDtypeStruct((some * heads, hd), jnp.float32),
             ),
-            in_specs=[SMEM, VMEM, ANY],
+            in_specs=[ANY, ANY, ANY],
             out_specs=(VMEM, VMEM),
             scratch_shapes=[
                 pltpu.VMEM((some, suffix_keys, 2 * hd), jnp.bfloat16),
                 pltpu.SemaphoreType.DMA((some,)),
+                pltpu.SMEM(ints.shape, jnp.int32),
+                pltpu.VMEM(queries.shape, queries.dtype),
                 pltpu.VMEM((some * heads, hd), jnp.float32),
                 pltpu.VMEM((some * heads, hd), jnp.float32),
+                pltpu.SemaphoreType.DMA,
+                pltpu.SemaphoreType.DMA,
             ],
-            compiler_params=limit(44),
+            compiler_params=limit(room),
             cost_estimate=pl.CostEstimate(
                 flops=4 * some * heads * suffix_keys * hd,
                 bytes_accessed=some * suffix_keys * 4 * hd,
                 transcendentals=some * heads * suffix_keys,
             ),
             name="suffix",
-        )(suffix_len, queries, suffix_cache.reshape(rows, suffix_keys, 2 * hd))
-
-    suffix_one = suffix(0)
-
-    kb, ct, sub = 2048, 256, 512
+        )(ints, queries_near, suffix_cache.reshape(rows, suffix_keys, 2 * hd))
+
+    suffix_one = suffix(0, 44)
+
+    kb, ct, sub = 2048, 512, 1024
     count = slots * heads
     partial = pl.pallas_call(
         functools.partial(prefix_kernel, kb=kb, ct=ct, sub=sub, scale=scale),
@@ -326,41 +377,52 @@
         concat_axis=0,
         tiled=True,
     )
-    suffix_two = suffix(some)
+    suffix_two = suffix(some, 44)
 
     attended = pl.pallas_call(
-        functools.partial(combine_kernel, capacity=capacity, heads=heads),
-        out_shape=jax.ShapeDtypeStruct((owners, rows, feat), jnp.bfloat16),
-        in_specs=[VMEM] * 7,
+        functools.partial(
+            combine_kernel, prefixes=prefixes, capacity=capacity, heads=heads
+        ),
+        out_shape=jax.ShapeDtypeStruct((rows, feat), jnp.bfloat16),
+        in_specs=[VMEM] * 6,
         out_specs=VMEM,
         compiler_params=limit(8),
         name="combine",
-    )(fork_row, slot_row, returned.reshape(places, feat // 2 + hd), *suffix_one, *suffix_two)
-    gathered = lax.all_to_all(attended, "owner", split_axis=0, concat_axis=0, tiled=True)
+    )(ints, returned.reshape(places, feat // 2 + hd), *suffix_one, *suffix_two)
+    copies = jnp.broadcast_to(attended[None], (owners, rows, feat))
+    gathered = lax.all_to_all(copies, "owner", split_axis=0, concat_axis=0, tiled=True)
 
     members = lax.axis_size("kv")
     chips = members // 2
-    place = lax.axis_index("kv")
-    chip, core = place // 2, place % 2
     block = owners * rows // members
     cols = out_weight.shape[1]
-    full = gathered.reshape(chips, 2, block, feat)
-    theirs = jnp.dot(
-        lax.dynamic_index_in_dim(full, 1 - core, 1, keepdims=False).reshape(chips * block, feat),
-        out_weight,
-        preferred_element_type=jnp.float32,
-    ).astype(jnp.bfloat16)
+    gathered = gathered.reshape(owners * rows, feat)
+
+    def project(other, dtype, name):
+        return pl.pallas_call(
+            functools.partial(project_kernel, other=other),
+            out_shape=jax.ShapeDtypeStruct((chips, block, cols), dtype),
+            in_specs=[VMEM, VMEM],
+            out_specs=VMEM,
+            compiler_params=limit(12),
+            name=name,
+        )(gathered, out_weight)
+
+    theirs = project(1, jnp.bfloat16, "project_theirs")
     from_pair = lax.ppermute(theirs, "kv", [(i, i ^ 1) for i in range(members)])
-    mine = jnp.dot(
-        lax.dynamic_index_in_dim(full, core, 1, keepdims=False).reshape(chips * block, feat),
-        out_weight,
-        preferred_element_type=jnp.float32,
-    )
-    pair_sum = (mine + from_pair.astype(jnp.float32)).reshape(chips, block, cols)
-    pair_sent = pair_sum.astype(jnp.bfloat16)
-    total = lax.dynamic_index_in_dim(pair_sum, chip, 0, keepdims=False)
-    for d in range(1, chips):
-        piece = lax.dynamic_index_in_dim(pair_sent, (chip + d) % chips, 0, keepdims=False)
+    mine = project(0, jnp.float32, "project_mine")
+    total, *pieces = pl.pallas_call(
+        pair_kernel,
+        out_shape=(
+            jax.ShapeDtypeStruct((block, cols), jnp.float32),
+            *[jax.ShapeDtypeStruct((block, cols), jnp.bfloat16)] * (chips - 1),
+        ),
+        in_specs=[VMEM, VMEM],
+        out_specs=(VMEM,) * chips,
+        compiler_params=limit(8),
+        name="pair",
+    )(mine, from_pair)
+    for d, piece in enumerate(pieces, 1):
         moved = lax.ppermute(
             piece,
             "kv",

time: 75.8 us -> 70.8 us (0.934)
  blocking collectives: 0 us -> 19.4 us
  waiting for transfers between devices: 28 us -> 11.5 us
  starting transfers between devices: 22.1 us -> 17.6 us
  Pallas kernels: 19.7 us -> 17.2 us
  matrix products: 0.87 us -> 0 us
    all_to_all x0 -> x1, blocking collectives: none -> 19.4 us  [body(): lax.all_to_all(copies, 'owner', split_axis=0, concat_axis=0, tiled=True)]
    all_to_all x1 -> x0, waiting for transfers between devices: 16.3 us -> none  [body(): lax.all_to_all(attended, 'owner', split_axis=0, concat_axis=0, tiled=True)]
    all_to_all x1 -> x0, starting transfers between devices: 3.83 us -> none  [body(): lax.all_to_all(attended, 'owner', split_axis=0, concat_axis=0, tiled=True)]
    ppermute x3, waiting for transfers between devices: 5.07 us -> 2.86 us  [body(): lax.ppermute(piece, 'kv', [(x * 2 + c, (x + d) % chips * 2 + c) for x in...]
    pallas_call x4 -> x7, Pallas kernels: 13.2 us -> 11.2 us  [the longest x2 8.59 us: suffix(): pl.pallas_call(functools.partial(suffix_kernel, first=first, skip=rows +...]
    all_to_all x1, waiting for transfers between devices: 1.74 us -> 3.67 us  [body(): lax.all_to_all(outgoing.reshape(owners, places // owners, feat // 2), 'ow...]
    all_to_all x1, starting transfers between devices: 5.48 us -> 3.62 us  [body(): lax.all_to_all(partial.reshape(owners, places // owners, feat // 2 + hd),...]
    ppermute x3, starting transfers between devices: 4.53 us -> 5.72 us  [body(): lax.ppermute(piece, 'kv', [(x * 2 + c, (x + d) % chips * 2 + c) for x in...]
  transfers between devices with their start and end apart: 7 -> 6, of which waited for: 7 -> 5; matrix products, arithmetic and copies ran while one was open for 0% -> 0% of each run, Pallas kernels for 13% -> 13%
where the time goes in v3:
time: 70.8 us; the launch traced here: 70.4 us
  blocking collectives  19.4 us (27%)
  starting transfers between devices  17.6 us (25%)
  Pallas kernels  17.2 us (24%)
  waiting for transfers between devices  11.5 us (16%)
  local copies, waits for them, and re-layouts  3.15 us (4%)
  other arithmetic  1.42 us (2%)
    all_to_all x1, blocking collectives, body(): lax.all_to_all(copies, 'owner', split_axis=0, concat_axis=0, tiled=True)  19.4 us
    pallas_call x2, Pallas kernels, suffix(): pl.pallas_call(functools.partial(suffix_kernel, first=first, skip=rows +...  8.59 us
    all_to_all x1, starting transfers between devices, body(): lax.all_to_all(outgoing.reshape(owners, places // owners, feat // 2), 'ow...  8.14 us
    pallas_call x1, Pallas kernels, body(): pl.pallas_call(functools.partial(prefix_kernel, kb=kb, ct=ct, sub=sub, sc...  6.07 us
    ppermute x3, starting transfers between devices, body(): lax.ppermute(piece, 'kv', [(x * 2 + c, (x + d) % chips * 2 + c) for x in...  5.72 us
    all_to_all x1, waiting for transfers between devices, body(): lax.all_to_all(partial.reshape(owners, places // owners, feat // 2 + hd),...  3.86 us
    all_to_all x1, waiting for transfers between devices, body(): lax.all_to_all(outgoing.reshape(owners, places // owners, feat // 2), 'ow...  3.67 us
    all_to_all x1, starting transfers between devices, body(): lax.all_to_all(partial.reshape(owners, places // owners, feat // 2 + hd),...  3.62 us
  transfers between devices with their start and end apart: 6, of which 5 were waited for; matrix products, arithmetic and copies ran while one was open for 0% of the time, Pallas kernels for 13%

profile of v3, /device:TPU:0, one launch (start us, length us, event | category | flops | bytes accessed | tf_op | source)
XLA Modules:
  0.0 70.4 jit_solution(9199496890617239558)
XLA Ops:
  0.0 0.8 %add_bitcast_fusion.ints_ref.len_hbm = s32[1,80]{1,0:T(1,128)S(1)} fusion(s32[32]{0:T(128)} %param.10, s32[16]{0:T(128)} %param.12, s32[32]{0:T(128)} %bitcast.17), kind=kLoop, calls=%fused_computation.1 | loop fusion | flops 160 | bytes 640 | tf_op jit(solution)/shard_map/reshape | solution.py:290
  0.8 0.0 copy-start.1
  0.8 0.8 %copy-done.1 = bf16[32,1024]{1,0:T(8,128)(2,1)S(1)} copy-done((bf16[32,1024]{1,0:T(8,128)(2,1)S(1)}, bf16[32,1024]{1,0:T(8,128)(2,1)}, u32[]{:S(2)}) %copy-start.1) | copy-done | bytes 65560
  1.6 1.0 %route.1 = (bf16[128,512]{1,0:T(8,128)(2,1)}, bf16[32,1024]{1,0:T(8,128)(2,1)S(1)}) custom-call(s32[1,80]{1,0:T(1,128)S(1)} %add_bitcast_fusion.ints_ref.len_hbm, bf16[32,1024]{1,0:T(8,128)(2,1)S(1)} %copy-done.1), custom_call_target="tpu_custom_call" | custom-call | tf_op jit(solution)/shard_map/route/pallas_call | solution.py:296
  2.7 8.1 %all-to-all-start = ((bf16[16,8,512]{2,1,0:T(8,128)(2,1)}), bf16[16,8,512]{2,1,0:T(8,128)(2,1)S(1)}, u32[]{:S(2)}, u32[]{:S(2)}) async-start(bf16[16,8,512]{2,1,0:T(8,128)(2,1)} %bitcast.2), calls=%async_computation | async-start | bytes 262144 | tf_op jit(solution)/shard_map/all_to_all | solution.py:307
  10.8 4.3 %suffix.2 = (f32[16,1024]{1,0:T(8,128)S(1)}, f32[128,128]{1,0:T(8,128)S(1)}) custom-call(s32[1,80]{1,0:T(1,128)S(1)} %add_bitcast_fusion.ints_ref.len_hbm, bf16[32,1024]{1,0:T(8,128)(2,1)S(1)} %get-tuple-element.16.q_hbm, bf16[32,1024,256]{2,1,0:T(8,128)(2,1)} %bitcast.15), custom_call_target="tpu_custom_call" | custom-call | flops 67108864 | bytes 8388608 | tf_op jit(solution)/shard_map/suffix/pallas_call | solution.py:319
  15.1 0.0 copy-start
  15.1 3.7 %all-to-all-done = bf16[16,8,512]{2,1,0:T(8,128)(2,1)S(1)} async-done(((bf16[16,8,512]{2,1,0:T(8,128)(2,1)}), bf16[16,8,512]{2,1,0:T(8,128)(2,1)S(1)}, u32[]{:S(2)}, u32[]{:S(2)}) %all-to-all-start) | async-done | bytes 131104 | tf_op jit(solution)/shard_map/all_to_all | solution.py:307
  18.8 0.0 copy-start.2
  18.8 2.2 %copy-done.2 = bf16[1,8192,1,256]{3,1,2,0:T(8,128)(2,1)S(1)} copy-done((bf16[1,8192,1,256]{3,1,2,0:T(8,128)(2,1)S(1)}, bf16[1,8192,1,256]{3,1,2,0:T(8,128)(2,1)}, u32[]{:S(2)}) %copy-start.2) | copy-done | bytes 4194328
  21.0 6.1 %prefix.1 = bf16[128,640]{1,0:T(8,128)(2,1)} custom-call(bf16[128,512]{1,0:T(8,128)(2,1)S(1)} %bitcast.13, bf16[8192,256]{1,0:T(8,128)(2,1)S(1)} %bitcast.14, f32[128,128]{1,0:T(8,128)S(1)} %get-tuple-element.17.after_ref.refs_1_), custom_call_target="tpu_custom_call" | custom-call | flops 2147483648 | bytes 4194304 | tf_op jit(solution)/shard_map/prefix/pallas_call | solution.py:350
  27.1 3.6 %all-to-all-start.1 = ((bf16[16,8,640]{2,1,0:T(8,128)(2,1)}), bf16[16,8,640]{2,1,0:T(8,128)(2,1)S(1)}, u32[]{:S(2)}, u32[]{:S(2)}) async-start(bf16[16,8,640]{2,1,0:T(8,128)(2,1)} %bitcast.6), calls=%async_computation.1 | async-start | bytes 327680 | tf_op jit(solution)/shard_map/all_to_all | solution.py:373
  30.7 4.3 %suffix.3 = (f32[16,1024]{1,0:T(8,128)S(1)}, f32[128,128]{1,0:T(8,128)S(1)}) custom-call(s32[1,80]{1,0:T(1,128)S(1)} %add_bitcast_fusion.ints_ref.len_hbm, bf16[32,1024]{1,0:T(8,128)(2,1)S(1)} %get-tuple-element.16.q_hbm, bf16[32,1024,256]{2,1,0:T(8,128)(2,1)} %bitcast.16), custom_call_target="tpu_custom_call" | custom-call | flops 67108864 | bytes 8388608 | tf_op jit(solution)/shard_map/suffix/pallas_call | solution.py:319
  35.0 3.9 %all-to-all-done.1 = bf16[16,8,640]{2,1,0:T(8,128)(2,1)S(1)} async-done(((bf16[16,8,640]{2,1,0:T(8,128)(2,1)}), bf16[16,8,640]{2,1,0:T(8,128)(2,1)S(1)}, u32[]{:S(2)}, u32[]{:S(2)}) %all-to-all-start.1) | async-done | bytes 163872 | tf_op jit(solution)/shard_map/all_to_all | solution.py:373
  38.8 0.6 combine.1
  39.5 0.1 broadcast_in_dim.2
  39.6 19.4 %all_to_all.15 = bf16[16,32,1024]{2,1,0:T(8,128)(2,1)S(1)} all-to-all(bf16[16,32,1024]{2,1,0:T(8,128)(2,1)S(1)} %broadcast_in_dim.2), channel_id=1, replica_groups=mesh['owner'=16,'kv'=8] {'owner'}, dimensions={0} | all-to-all | bytes 2097152 | tf_op jit(solution)/shard_map/all_to_all | solution.py:393
  59.0 0.0 copy-done
  59.0 0.4 project_theirs.1
  59.5 0.1 collective-permute-start
  59.6 0.4 project_mine.1.mine_ref
  60.0 1.1 %collective-permute-done.other_ref = bf16[4,64,512]{2,1,0:T(8,128)(2,1)S(1)} collective-permute-done((bf16[4,64,512]{2,1,0:T(8,128)(2,1)S(1)}, bf16[4,64,512]{2,1,0:T(8,128)(2,1)S(1)}, u32[]{:S(2)}, u32[]{:S(2)}) %collective-permute-start) | collective-permute-done | bytes 262176 | tf_op jit(solution)/shard_map/ppermute | solution.py:412
  61.1 1.6 %collective-permute-start.1 = (bf16[64,512]{1,0:T(8,128)(2,1)S(1)}, bf16[64,512]{1,0:T(8,128)(2,1)S(1)}, u32[]{:S(2)}, u32[]{:S(2)}) collective-permute-start(bf16[64,512]{1,0:T(8,128)(2,1)S(1)} %get-tuple-element.22), channel_id=1, source_target_pairs={{0,2},{1,3},{2,4},{3,5},{4,6},{5,7},{6,0},{7,1},{8,10},{9,11},{10,... | collective-permute-start | bytes 196616 | tf_op jit(solution)/shard_map/ppermute | solution.py:426
  62.7 2.8 %collective-permute-start.2 = (bf16[64,512]{1,0:T(8,128)(2,1)S(1)}, bf16[64,512]{1,0:T(8,128)(2,1)S(1)}, u32[]{:S(2)}, u32[]{:S(2)}) collective-permute-start(bf16[64,512]{1,0:T(8,128)(2,1)S(1)} %get-tuple-element.23), channel_id=1, source_target_pairs={{0,4},{1,5},{2,6},{3,7},{4,0},{5,1},{6,2},{7,3},{8,12},{9,13},{10,... | collective-permute-start | bytes 196616 | tf_op jit(solution)/shard_map/ppermute | solution.py:426
  65.4 1.4 %collective-permute-start.3 = (bf16[64,512]{1,0:T(8,128)(2,1)S(1)}, bf16[64,512]{1,0:T(8,128)(2,1)S(1)}, u32[]{:S(2)}, u32[]{:S(2)}) collective-permute-start(bf16[64,512]{1,0:T(8,128)(2,1)S(1)} %get-tuple-element.24), channel_id=1, source_target_pairs={{0,6},{1,7},{2,0},{3,1},{4,2},{5,3},{6,4},{7,5},{8,14},{9,15},{10,... | collective-permute-start | bytes 196616 | tf_op jit(solution)/shard_map/ppermute | solution.py:426
  66.8 0.0 collective-permute-done.1
  66.8 2.1 %collective-permute-done.2 = bf16[64,512]{1,0:T(8,128)(2,1)S(1)} collective-permute-done((bf16[64,512]{1,0:T(8,128)(2,1)S(1)}, bf16[64,512]{1,0:T(8,128)(2,1)S(1)}, u32[]{:S(2)}, u32[]{:S(2)}) %collective-permute-start.2) | collective-permute-done | bytes 65568 | tf_op jit(solution)/shard_map/ppermute | solution.py:426
  69.0 0.8 %collective-permute-done.3 = bf16[64,512]{1,0:T(8,128)(2,1)S(1)} collective-permute-done((bf16[64,512]{1,0:T(8,128)(2,1)S(1)}, bf16[64,512]{1,0:T(8,128)(2,1)S(1)}, u32[]{:S(2)}, u32[]{:S(2)}) %collective-permute-start.3) | collective-permute-done | bytes 65568 | tf_op jit(solution)/shard_map/ppermute | solution.py:426
  69.7 0.7 add_convert_fusion
  (1 shorter events, 0.0 us)
Async XLA Ops:
  0.8 0.8 %copy-start.1 = (bf16[32,1024]{1,0:T(8,128)(2,1)S(1)}, bf16[32,1024]{1,0:T(8,128)(2,1)}, u32[]{:S(2)}) copy-start(bf16[32,1024]{1,0:T(8,128)(2,1)} %query_ref.1) | copy-start | bytes 196612
  2.7 16.1 %all-to-all-start = ((bf16[16,8,512]{2,1,0:T(8,128)(2,1)}), bf16[16,8,512]{2,1,0:T(8,128)(2,1)S(1)}, u32[]{:S(2)}, u32[]{:S(2)}) async-start(bf16[16,8,512]{2,1,0:T(8,128)(2,1)} %bitcast.2), calls=%async_computation | async-start | bytes 262144 | tf_op jit(solution)/shard_map/all_to_all | solution.py:307
  15.1 43.9 %copy-start = (bf16[1024,512]{1,0:T(8,128)(2,1)S(1)}, bf16[1024,512]{1,0:T(8,128)(2,1)}, u32[]{:S(2)}) copy-start(bf16[1024,512]{1,0:T(8,128)(2,1)} %weight_ref.3) | copy-start | bytes 3145732
  18.8 2.2 %copy-start.2 = (bf16[1,8192,1,256]{3,1,2,0:T(8,128)(2,1)S(1)}, bf16[1,8192,1,256]{3,1,2,0:T(8,128)(2,1)}, u32[]{:S(2)}) copy-start(bf16[1,8192,1,256]{3,1,2,0:T(8,128)(2,1)} %param.8) | copy-start | bytes 12582916
  27.1 11.8 %all-to-all-start.1 = ((bf16[16,8,640]{2,1,0:T(8,128)(2,1)}), bf16[16,8,640]{2,1,0:T(8,128)(2,1)S(1)}, u32[]{:S(2)}, u32[]{:S(2)}) async-start(bf16[16,8,640]{2,1,0:T(8,128)(2,1)} %bitcast.6), calls=%async_computation.1 | async-start | bytes 327680 | tf_op jit(solution)/shard_map/all_to_all | solution.py:373
  59.5 1.6 %collective-permute-start = (bf16[4,64,512]{2,1,0:T(8,128)(2,1)S(1)}, bf16[4,64,512]{2,1,0:T(8,128)(2,1)S(1)}, u32[]{:S(2)}, u32[]{:S(2)}) collective-permute-start(bf16[4,64,512]{2,1,0:T(8,128)(2,1)S(1)} %project_theirs.1), channel_id=1, source_target_pairs={{0,1},{1,0},{2,3},{3,2},{4,5},{5,4},{6,7},{7,6},{8,9},{9,8},{10,11... | collective-permute-start | bytes 786440 | tf_op jit(solution)/shard_map/ppermute | solution.py:412
  61.1 5.7 %collective-permute-start.1 = (bf16[64,512]{1,0:T(8,128)(2,1)S(1)}, bf16[64,512]{1,0:T(8,128)(2,1)S(1)}, u32[]{:S(2)}, u32[]{:S(2)}) collective-permute-start(bf16[64,512]{1,0:T(8,128)(2,1)S(1)} %get-tuple-element.22), channel_id=1, source_target_pairs={{0,2},{1,3},{2,4},{3,5},{4,6},{5,7},{6,0},{7,1},{8,10},{9,11},{10,... | collective-permute-start | bytes 196616 | tf_op jit(solution)/shard_map/ppermute | solution.py:426
  62.7 6.3 %collective-permute-start.2 = (bf16[64,512]{1,0:T(8,128)(2,1)S(1)}, bf16[64,512]{1,0:T(8,128)(2,1)S(1)}, u32[]{:S(2)}, u32[]{:S(2)}) collective-permute-start(bf16[64,512]{1,0:T(8,128)(2,1)S(1)} %get-tuple-element.23), channel_id=1, source_target_pairs={{0,4},{1,5},{2,6},{3,7},{4,0},{5,1},{6,2},{7,3},{8,12},{9,13},{10,... | collective-permute-start | bytes 196616 | tf_op jit(solution)/shard_map/ppermute | solution.py:426
  65.4 4.3 %collective-permute-start.3 = (bf16[64,512]{1,0:T(8,128)(2,1)S(1)}, bf16[64,512]{1,0:T(8,128)(2,1)S(1)}, u32[]{:S(2)}, u32[]{:S(2)}) collective-permute-start(bf16[64,512]{1,0:T(8,128)(2,1)S(1)} %get-tuple-element.24), channel_id=1, source_target_pairs={{0,6},{1,7},{2,0},{3,1},{4,2},{5,3},{6,4},{7,5},{8,14},{9,15},{10,... | collective-permute-start | bytes 196616 | tf_op jit(solution)/shard_map/ppermute | solution.py:426

commit v4 on v3

--- a/solution.py
+++ b/solution.py
@@ -14,6 +14,7 @@
 ANY = pl.BlockSpec(memory_space=pl.ANY)
 MIB = 2**20
 GROUP_ROWS = 4
+PREFIX_MIB = 52
 
 
 def one_hot_slots(ints_ref, rows, prefixes, capacity):
@@ -154,7 +155,7 @@
 
 
 def prefix_kernel(
-    x_ref, kv, after_ref, out_ref, q_s, s_s, acc_s, vt_s, *, kb, ct, sub, scale
+    x_ref, kv_hbm, after_ref, out_ref, kv, sems, q_s, s_s, acc_s, vt_s, *, kb, ct, sub, scale
 ):
     keys = kv.shape[0]
     hd = kv.shape[1] // 2
@@ -162,6 +163,13 @@
     heads = feat // hd
     count = slots * heads
     c2 = scale * LOG2E
+
+    def copy_of(c):
+        part = pl.ds(c * kb, kb)
+        return pltpu.make_async_copy(kv_hbm.at[part], kv.at[part], sems.at[c])
+
+    for c in range(keys // kb):
+        copy_of(c).start()
     qf = jnp.concatenate([x_ref[:, h * hd : (h + 1) * hd] for h in range(heads)], axis=0)
     qf = qf.astype(jnp.float32).T * c2
     hi = qf.astype(jnp.bfloat16)
@@ -174,6 +182,8 @@
 
     def scores(idx, j, highest):
         c, t = items[idx]
+        if j == 0 and t == 0:
+            copy_of(c).wait()
         here = slice(c * kb + j * sub, c * kb + (j + 1) * sub)
         k = kv[here, :hd]
         s = jnp.dot(
@@ -345,20 +355,22 @@
 
     suffix_one = suffix(0, 44)
 
-    kb, ct, sub = 2048, 512, 1024
+    kb, ct, sub = 1024, 512, 1024
     count = slots * heads
     partial = pl.pallas_call(
         functools.partial(prefix_kernel, kb=kb, ct=ct, sub=sub, scale=scale),
         out_shape=jax.ShapeDtypeStruct((places, feat // 2 + hd), jnp.bfloat16),
-        in_specs=[VMEM, VMEM, ANY],
+        in_specs=[VMEM, ANY, ANY],
         out_specs=VMEM,
         scratch_shapes=[
+            pltpu.VMEM((keys, 2 * hd), jnp.bfloat16),
+            pltpu.SemaphoreType.DMA((keys // kb,)),
             pltpu.VMEM((2 * hd, count), jnp.bfloat16),
             pltpu.VMEM((2, kb, ct), jnp.float32),
             pltpu.VMEM((hd + 16, count), jnp.float32),
             pltpu.VMEM((2, hd + 16, kb), jnp.bfloat16),
         ],
-        compiler_params=limit(24),
+        compiler_params=limit(PREFIX_MIB),
         cost_estimate=pl.CostEstimate(
             flops=4 * count * keys * hd,
             bytes_accessed=keys * 4 * hd,

time: 70.8 us -> 69.9 us (0.987)
  local copies, waits for them, and re-layouts: 3.15 us -> 0.96 us
  Pallas kernels: 17.2 us -> 18.6 us
    unnamed x6 -> x4, local copies, waits for them, and re-layouts: 3.03 us -> 0.85 us
    pallas_call x1, Pallas kernels: 6.07 us -> 7.4 us  [body(): pl.pallas_call(functools.partial(prefix_kernel, kb=kb, ct=ct, sub=sub, sc...]
where the time goes in v4:
time: 69.9 us; the launch traced here: 69.5 us
  blocking collectives  19.4 us (28%)
  Pallas kernels  18.6 us (27%)
  starting transfers between devices  17.6 us (25%)
  waiting for transfers between devices  11.5 us (16%)
  other arithmetic  1.42 us (2%)
  local copies, waits for them, and re-layouts  0.96 us (1%)
    all_to_all x1, blocking collectives, body(): lax.all_to_all(copies, 'owner', split_axis=0, concat_axis=0, tiled=True)  19.4 us
    pallas_call x2, Pallas kernels, suffix(): pl.pallas_call(functools.partial(suffix_kernel, first=first, skip=rows +...  8.59 us
    all_to_all x1, starting transfers between devices, body(): lax.all_to_all(outgoing.reshape(owners, places // owners, feat // 2), 'ow...  8.14 us
    pallas_call x1, Pallas kernels, body(): pl.pallas_call(functools.partial(prefix_kernel, kb=kb, ct=ct, sub=sub, sc...  7.4 us
    ppermute x3, starting transfers between devices, body(): lax.ppermute(piece, 'kv', [(x * 2 + c, (x + d) % chips * 2 + c) for x in...  5.72 us
    all_to_all x1, waiting for transfers between devices, body(): lax.all_to_all(partial.reshape(owners, places // owners, feat // 2 + hd),...  3.86 us
    all_to_all x1, waiting for transfers between devices, body(): lax.all_to_all(outgoing.reshape(owners, places // owners, feat // 2), 'ow...  3.67 us
    all_to_all x1, starting transfers between devices, body(): lax.all_to_all(partial.reshape(owners, places // owners, feat // 2 + hd),...  3.64 us
  transfers between devices with their start and end apart: 6, of which 5 were waited for; matrix products, arithmetic and copies ran while one was open for 0% of the time, Pallas kernels for 13%

profile of v4, /device:TPU:0, one launch (start us, length us, event | category | flops | bytes accessed | tf_op | source)
XLA Modules:
  0.0 69.5 jit_solution(7095900632987399815)
XLA Ops:
  0.0 0.8 %add_bitcast_fusion.ints_ref.len_hbm = s32[1,80]{1,0:T(1,128)S(1)} fusion(s32[32]{0:T(128)} %param.10, s32[16]{0:T(128)} %param.12, s32[32]{0:T(128)} %bitcast.16), kind=kLoop, calls=%fused_computation.1 | loop fusion | flops 160 | bytes 640 | tf_op jit(solution)/shard_map/reshape | solution.py:300
  0.8 0.0 copy-start.1
  0.8 0.8 %copy-done.1 = bf16[32,1024]{1,0:T(8,128)(2,1)S(1)} copy-done((bf16[32,1024]{1,0:T(8,128)(2,1)S(1)}, bf16[32,1024]{1,0:T(8,128)(2,1)}, u32[]{:S(2)}) %copy-start.1) | copy-done | bytes 65560
  1.6 1.0 %route.1 = (bf16[128,512]{1,0:T(8,128)(2,1)}, bf16[32,1024]{1,0:T(8,128)(2,1)S(1)}) custom-call(s32[1,80]{1,0:T(1,128)S(1)} %add_bitcast_fusion.ints_ref.len_hbm, bf16[32,1024]{1,0:T(8,128)(2,1)S(1)} %copy-done.1), custom_call_target="tpu_custom_call" | custom-call | tf_op jit(solution)/shard_map/route/pallas_call | solution.py:306
  2.7 8.1 %all-to-all-start = ((bf16[16,8,512]{2,1,0:T(8,128)(2,1)}), bf16[16,8,512]{2,1,0:T(8,128)(2,1)S(1)}, u32[]{:S(2)}, u32[]{:S(2)}) async-start(bf16[16,8,512]{2,1,0:T(8,128)(2,1)} %bitcast.2), calls=%async_computation | async-start | bytes 262144 | tf_op jit(solution)/shard_map/all_to_all | solution.py:317
  10.8 4.3 %suffix.2 = (f32[16,1024]{1,0:T(8,128)S(1)}, f32[128,128]{1,0:T(8,128)S(1)}) custom-call(s32[1,80]{1,0:T(1,128)S(1)} %add_bitcast_fusion.ints_ref.len_hbm, bf16[32,1024]{1,0:T(8,128)(2,1)S(1)} %get-tuple-element.16.q_hbm, bf16[32,1024,256]{2,1,0:T(8,128)(2,1)} %bitcast.14), custom_call_target="tpu_custom_call" | custom-call | flops 67108864 | bytes 8388608 | tf_op jit(solution)/shard_map/suffix/pallas_call | solution.py:329
  15.1 0.0 copy-start
  15.1 3.7 %all-to-all-done = bf16[16,8,512]{2,1,0:T(8,128)(2,1)S(1)} async-done(((bf16[16,8,512]{2,1,0:T(8,128)(2,1)}), bf16[16,8,512]{2,1,0:T(8,128)(2,1)S(1)}, u32[]{:S(2)}, u32[]{:S(2)}) %all-to-all-start) | async-done | bytes 131104 | tf_op jit(solution)/shard_map/all_to_all | solution.py:317
  18.8 7.4 %prefix.1 = bf16[128,640]{1,0:T(8,128)(2,1)} custom-call(bf16[128,512]{1,0:T(8,128)(2,1)S(1)} %bitcast.13, bf16[8192,256]{1,0:T(8,128)(2,1)} %bitcast.17, f32[128,128]{1,0:T(8,128)S(1)} %get-tuple-element.17.after_ref.refs_1_), custom_call_target="tpu_custom_call" | custom-call | flops 2147483648 | bytes 4194304 | tf_op jit(solution)/shard_map/prefix/pallas_call | solution.py:360
  26.2 3.6 %all-to-all-start.1 = ((bf16[16,8,640]{2,1,0:T(8,128)(2,1)}), bf16[16,8,640]{2,1,0:T(8,128)(2,1)S(1)}, u32[]{:S(2)}, u32[]{:S(2)}) async-start(bf16[16,8,640]{2,1,0:T(8,128)(2,1)} %bitcast.6), calls=%async_computation.1 | async-start | bytes 327680 | tf_op jit(solution)/shard_map/all_to_all | solution.py:385
  29.8 4.3 %suffix.3 = (f32[16,1024]{1,0:T(8,128)S(1)}, f32[128,128]{1,0:T(8,128)S(1)}) custom-call(s32[1,80]{1,0:T(1,128)S(1)} %add_bitcast_fusion.ints_ref.len_hbm, bf16[32,1024]{1,0:T(8,128)(2,1)S(1)} %get-tuple-element.16.q_hbm, bf16[32,1024,256]{2,1,0:T(8,128)(2,1)} %bitcast.15), custom_call_target="tpu_custom_call" | custom-call | flops 67108864 | bytes 8388608 | tf_op jit(solution)/shard_map/suffix/pallas_call | solution.py:329
  34.1 3.9 %all-to-all-done.1 = bf16[16,8,640]{2,1,0:T(8,128)(2,1)S(1)} async-done(((bf16[16,8,640]{2,1,0:T(8,128)(2,1)}), bf16[16,8,640]{2,1,0:T(8,128)(2,1)S(1)}, u32[]{:S(2)}, u32[]{:S(2)}) %all-to-all-start.1) | async-done | bytes 163872 | tf_op jit(solution)/shard_map/all_to_all | solution.py:385
  38.0 0.6 combine.1
  38.6 0.1 broadcast_in_dim.2
  38.8 19.4 %all_to_all.15 = bf16[16,32,1024]{2,1,0:T(8,128)(2,1)S(1)} all-to-all(bf16[16,32,1024]{2,1,0:T(8,128)(2,1)S(1)} %broadcast_in_dim.2), channel_id=1, replica_groups=mesh['owner'=16,'kv'=8] {'owner'}, dimensions={0} | all-to-all | bytes 2097152 | tf_op jit(solution)/shard_map/all_to_all | solution.py:405
  58.2 0.0 copy-done
  58.2 0.4 project_theirs.1
  58.6 0.1 collective-permute-start
  58.7 0.4 project_mine.1.mine_ref
  59.2 1.1 %collective-permute-done.other_ref = bf16[4,64,512]{2,1,0:T(8,128)(2,1)S(1)} collective-permute-done((bf16[4,64,512]{2,1,0:T(8,128)(2,1)S(1)}, bf16[4,64,512]{2,1,0:T(8,128)(2,1)S(1)}, u32[]{:S(2)}, u32[]{:S(2)}) %collective-permute-start) | collective-permute-done | bytes 262176 | tf_op jit(solution)/shard_map/ppermute | solution.py:424
  60.3 1.5 %collective-permute-start.1 = (bf16[64,512]{1,0:T(8,128)(2,1)S(1)}, bf16[64,512]{1,0:T(8,128)(2,1)S(1)}, u32[]{:S(2)}, u32[]{:S(2)}) collective-permute-start(bf16[64,512]{1,0:T(8,128)(2,1)S(1)} %get-tuple-element.22), channel_id=1, source_target_pairs={{0,2},{1,3},{2,4},{3,5},{4,6},{5,7},{6,0},{7,1},{8,10},{9,11},{10,... | collective-permute-start | bytes 196616 | tf_op jit(solution)/shard_map/ppermute | solution.py:438
  61.8 2.7 %collective-permute-start.2 = (bf16[64,512]{1,0:T(8,128)(2,1)S(1)}, bf16[64,512]{1,0:T(8,128)(2,1)S(1)}, u32[]{:S(2)}, u32[]{:S(2)}) collective-permute-start(bf16[64,512]{1,0:T(8,128)(2,1)S(1)} %get-tuple-element.23), channel_id=1, source_target_pairs={{0,4},{1,5},{2,6},{3,7},{4,0},{5,1},{6,2},{7,3},{8,12},{9,13},{10,... | collective-permute-start | bytes 196616 | tf_op jit(solution)/shard_map/ppermute | solution.py:438
  64.6 1.4 %collective-permute-start.3 = (bf16[64,512]{1,0:T(8,128)(2,1)S(1)}, bf16[64,512]{1,0:T(8,128)(2,1)S(1)}, u32[]{:S(2)}, u32[]{:S(2)}) collective-permute-start(bf16[64,512]{1,0:T(8,128)(2,1)S(1)} %get-tuple-element.24), channel_id=1, source_target_pairs={{0,6},{1,7},{2,0},{3,1},{4,2},{5,3},{6,4},{7,5},{8,14},{9,15},{10,... | collective-permute-start | bytes 196616 | tf_op jit(solution)/shard_map/ppermute | solution.py:438
  66.0 0.0 collective-permute-done.1
  66.0 2.1 %collective-permute-done.2 = bf16[64,512]{1,0:T(8,128)(2,1)S(1)} collective-permute-done((bf16[64,512]{1,0:T(8,128)(2,1)S(1)}, bf16[64,512]{1,0:T(8,128)(2,1)S(1)}, u32[]{:S(2)}, u32[]{:S(2)}) %collective-permute-start.2) | collective-permute-done | bytes 65568 | tf_op jit(solution)/shard_map/ppermute | solution.py:438
  68.1 0.8 %collective-permute-done.3 = bf16[64,512]{1,0:T(8,128)(2,1)S(1)} collective-permute-done((bf16[64,512]{1,0:T(8,128)(2,1)S(1)}, bf16[64,512]{1,0:T(8,128)(2,1)S(1)}, u32[]{:S(2)}, u32[]{:S(2)}) %collective-permute-start.3) | collective-permute-done | bytes 65568 | tf_op jit(solution)/shard_map/ppermute | solution.py:438
  68.9 0.7 add_convert_fusion
  (1 shorter events, 0.0 us)
Async XLA Ops:
  0.8 0.8 %copy-start.1 = (bf16[32,1024]{1,0:T(8,128)(2,1)S(1)}, bf16[32,1024]{1,0:T(8,128)(2,1)}, u32[]{:S(2)}) copy-start(bf16[32,1024]{1,0:T(8,128)(2,1)} %query_ref.1) | copy-start | bytes 196612
  2.7 16.1 %all-to-all-start = ((bf16[16,8,512]{2,1,0:T(8,128)(2,1)}), bf16[16,8,512]{2,1,0:T(8,128)(2,1)S(1)}, u32[]{:S(2)}, u32[]{:S(2)}) async-start(bf16[16,8,512]{2,1,0:T(8,128)(2,1)} %bitcast.2), calls=%async_computation | async-start | bytes 262144 | tf_op jit(solution)/shard_map/all_to_all | solution.py:317
  15.1 43.1 %copy-start = (bf16[1024,512]{1,0:T(8,128)(2,1)S(1)}, bf16[1024,512]{1,0:T(8,128)(2,1)}, u32[]{:S(2)}) copy-start(bf16[1024,512]{1,0:T(8,128)(2,1)} %weight_ref.3) | copy-start | bytes 3145732
  26.2 11.8 %all-to-all-start.1 = ((bf16[16,8,640]{2,1,0:T(8,128)(2,1)}), bf16[16,8,640]{2,1,0:T(8,128)(2,1)S(1)}, u32[]{:S(2)}, u32[]{:S(2)}) async-start(bf16[16,8,640]{2,1,0:T(8,128)(2,1)} %bitcast.6), calls=%async_computation.1 | async-start | bytes 327680 | tf_op jit(solution)/shard_map/all_to_all | solution.py:385
  58.6 1.6 %collective-permute-start = (bf16[4,64,512]{2,1,0:T(8,128)(2,1)S(1)}, bf16[4,64,512]{2,1,0:T(8,128)(2,1)S(1)}, u32[]{:S(2)}, u32[]{:S(2)}) collective-permute-start(bf16[4,64,512]{2,1,0:T(8,128)(2,1)S(1)} %project_theirs.1), channel_id=1, source_target_pairs={{0,1},{1,0},{2,3},{3,2},{4,5},{5,4},{6,7},{7,6},{8,9},{9,8},{10,11... | collective-permute-start | bytes 786440 | tf_op jit(solution)/shard_map/ppermute | solution.py:424
  60.3 5.7 %collective-permute-start.1 = (bf16[64,512]{1,0:T(8,128)(2,1)S(1)}, bf16[64,512]{1,0:T(8,128)(2,1)S(1)}, u32[]{:S(2)}, u32[]{:S(2)}) collective-permute-start(bf16[64,512]{1,0:T(8,128)(2,1)S(1)} %get-tuple-element.22), channel_id=1, source_target_pairs={{0,2},{1,3},{2,4},{3,5},{4,6},{5,7},{6,0},{7,1},{8,10},{9,11},{10,... | collective-permute-start | bytes 196616 | tf_op jit(solution)/shard_map/ppermute | solution.py:438
  61.8 6.3 %collective-permute-start.2 = (bf16[64,512]{1,0:T(8,128)(2,1)S(1)}, bf16[64,512]{1,0:T(8,128)(2,1)S(1)}, u32[]{:S(2)}, u32[]{:S(2)}) collective-permute-start(bf16[64,512]{1,0:T(8,128)(2,1)S(1)} %get-tuple-element.23), channel_id=1, source_target_pairs={{0,4},{1,5},{2,6},{3,7},{4,0},{5,1},{6,2},{7,3},{8,12},{9,13},{10,... | collective-permute-start | bytes 196616 | tf_op jit(solution)/shard_map/ppermute | solution.py:438
  64.6 4.3 %collective-permute-start.3 = (bf16[64,512]{1,0:T(8,128)(2,1)S(1)}, bf16[64,512]{1,0:T(8,128)(2,1)S(1)}, u32[]{:S(2)}, u32[]{:S(2)}) collective-permute-start(bf16[64,512]{1,0:T(8,128)(2,1)S(1)} %get-tuple-element.24), channel_id=1, source_target_pairs={{0,6},{1,7},{2,0},{3,1},{4,2},{5,3},{6,4},{7,5},{8,14},{9,15},{10,... | collective-permute-start | bytes 196616 | tf_op jit(solution)/shard_map/ppermute | solution.py:438

commit v5 on v4

--- a/solution.py
+++ b/solution.py
@@ -164,11 +164,16 @@
     count = slots * heads
     c2 = scale * LOG2E
 
+    pieces_at, begin = {}, 0
+    while begin < keys // kb:
+        pieces_at[begin] = max(1, begin)
+        begin += pieces_at[begin]
+
     def copy_of(c):
-        part = pl.ds(c * kb, kb)
+        part = pl.ds(c * kb, min(pieces_at[c], keys // kb - c) * kb)
         return pltpu.make_async_copy(kv_hbm.at[part], kv.at[part], sems.at[c])
 
-    for c in range(keys // kb):
+    for c in pieces_at:
         copy_of(c).start()
     qf = jnp.concatenate([x_ref[:, h * hd : (h + 1) * hd] for h in range(heads)], axis=0)
     qf = qf.astype(jnp.float32).T * c2
@@ -182,7 +187,7 @@
 
     def scores(idx, j, highest):
         c, t = items[idx]
-        if j == 0 and t == 0:
+        if j == 0 and t == 0 and c in pieces_at:
             copy_of(c).wait()
         here = slice(c * kb + j * sub, c * kb + (j + 1) * sub)
         k = kv[here, :hd]

time: 69.9 us -> 70 us (level)
  no operation moved by 1% of the time
where the time goes in v5:
time: 70 us; the launch traced here: 69.6 us
  blocking collectives  19.4 us (28%)
  Pallas kernels  18.7 us (27%)
  starting transfers between devices  17.6 us (25%)
  waiting for transfers between devices  11.5 us (16%)
  other arithmetic  1.42 us (2%)
  local copies, waits for them, and re-layouts  0.96 us (1%)
    all_to_all x1, blocking collectives, body(): lax.all_to_all(copies, 'owner', split_axis=0, concat_axis=0, tiled=True)  19.4 us
    pallas_call x2, Pallas kernels, suffix(): pl.pallas_call(functools.partial(suffix_kernel, first=first, skip=rows +...  8.59 us
    all_to_all x1, starting transfers between devices, body(): lax.all_to_all(outgoing.reshape(owners, places // owners, feat // 2), 'ow...  8.14 us
    pallas_call x1, Pallas kernels, body(): pl.pallas_call(functools.partial(prefix_kernel, kb=kb, ct=ct, sub=sub, sc...  7.49 us
    ppermute x3, starting transfers between devices, body(): lax.ppermute(piece, 'kv', [(x * 2 + c, (x + d) % chips * 2 + c) for x in...  5.72 us
    all_to_all x1, waiting for transfers between devices, body(): lax.all_to_all(partial.reshape(owners, places // owners, feat // 2 + hd),...  3.86 us
    all_to_all x1, waiting for transfers between devices, body(): lax.all_to_all(outgoing.reshape(owners, places // owners, feat // 2), 'ow...  3.67 us
    all_to_all x1, starting transfers between devices, body(): lax.all_to_all(partial.reshape(owners, places // owners, feat // 2 + hd),...  3.64 us
  transfers between devices with their start and end apart: 6, of which 5 were waited for; matrix products, arithmetic and copies ran while one was open for 0% of the time, Pallas kernels for 13%

profile of v5, /device:TPU:0, one launch (start us, length us, event | category | flops | bytes accessed | tf_op | source)
XLA Modules:
  0.0 69.6 jit_solution(10506244911818392234)
XLA Ops:
  0.0 0.8 %add_bitcast_fusion.ints_ref.len_hbm = s32[1,80]{1,0:T(1,128)S(1)} fusion(s32[32]{0:T(128)} %param.10, s32[16]{0:T(128)} %param.12, s32[32]{0:T(128)} %bitcast.16), kind=kLoop, calls=%fused_computation.1 | loop fusion | flops 160 | bytes 640 | tf_op jit(solution)/shard_map/reshape | solution.py:305
  0.8 0.0 copy-start.1
  0.8 0.8 %copy-done.1 = bf16[32,1024]{1,0:T(8,128)(2,1)S(1)} copy-done((bf16[32,1024]{1,0:T(8,128)(2,1)S(1)}, bf16[32,1024]{1,0:T(8,128)(2,1)}, u32[]{:S(2)}) %copy-start.1) | copy-done | bytes 65560
  1.6 1.0 %route.1 = (bf16[128,512]{1,0:T(8,128)(2,1)}, bf16[32,1024]{1,0:T(8,128)(2,1)S(1)}) custom-call(s32[1,80]{1,0:T(1,128)S(1)} %add_bitcast_fusion.ints_ref.len_hbm, bf16[32,1024]{1,0:T(8,128)(2,1)S(1)} %copy-done.1), custom_call_target="tpu_custom_call" | custom-call | tf_op jit(solution)/shard_map/route/pallas_call | solution.py:311
  2.7 8.1 %all-to-all-start = ((bf16[16,8,512]{2,1,0:T(8,128)(2,1)}), bf16[16,8,512]{2,1,0:T(8,128)(2,1)S(1)}, u32[]{:S(2)}, u32[]{:S(2)}) async-start(bf16[16,8,512]{2,1,0:T(8,128)(2,1)} %bitcast.2), calls=%async_computation | async-start | bytes 262144 | tf_op jit(solution)/shard_map/all_to_all | solution.py:322
  10.8 4.3 %suffix.2 = (f32[16,1024]{1,0:T(8,128)S(1)}, f32[128,128]{1,0:T(8,128)S(1)}) custom-call(s32[1,80]{1,0:T(1,128)S(1)} %add_bitcast_fusion.ints_ref.len_hbm, bf16[32,1024]{1,0:T(8,128)(2,1)S(1)} %get-tuple-element.16.q_hbm, bf16[32,1024,256]{2,1,0:T(8,128)(2,1)} %bitcast.14), custom_call_target="tpu_custom_call" | custom-call | flops 67108864 | bytes 8388608 | tf_op jit(solution)/shard_map/suffix/pallas_call | solution.py:334
  15.1 0.0 copy-start
  15.1 3.7 %all-to-all-done = bf16[16,8,512]{2,1,0:T(8,128)(2,1)S(1)} async-done(((bf16[16,8,512]{2,1,0:T(8,128)(2,1)}), bf16[16,8,512]{2,1,0:T(8,128)(2,1)S(1)}, u32[]{:S(2)}, u32[]{:S(2)}) %all-to-all-start) | async-done | bytes 131104 | tf_op jit(solution)/shard_map/all_to_all | solution.py:322
  18.8 7.5 %prefix.1 = bf16[128,640]{1,0:T(8,128)(2,1)} custom-call(bf16[128,512]{1,0:T(8,128)(2,1)S(1)} %bitcast.13, bf16[8192,256]{1,0:T(8,128)(2,1)} %bitcast.17, f32[128,128]{1,0:T(8,128)S(1)} %get-tuple-element.17.after_ref.refs_1_), custom_call_target="tpu_custom_call" | custom-call | flops 2147483648 | bytes 4194304 | tf_op jit(solution)/shard_map/prefix/pallas_call | solution.py:365
  26.3 3.6 %all-to-all-start.1 = ((bf16[16,8,640]{2,1,0:T(8,128)(2,1)}), bf16[16,8,640]{2,1,0:T(8,128)(2,1)S(1)}, u32[]{:S(2)}, u32[]{:S(2)}) async-start(bf16[16,8,640]{2,1,0:T(8,128)(2,1)} %bitcast.6), calls=%async_computation.1 | async-start | bytes 327680 | tf_op jit(solution)/shard_map/all_to_all | solution.py:390
  29.9 4.3 %suffix.3 = (f32[16,1024]{1,0:T(8,128)S(1)}, f32[128,128]{1,0:T(8,128)S(1)}) custom-call(s32[1,80]{1,0:T(1,128)S(1)} %add_bitcast_fusion.ints_ref.len_hbm, bf16[32,1024]{1,0:T(8,128)(2,1)S(1)} %get-tuple-element.16.q_hbm, bf16[32,1024,256]{2,1,0:T(8,128)(2,1)} %bitcast.15), custom_call_target="tpu_custom_call" | custom-call | flops 67108864 | bytes 8388608 | tf_op jit(solution)/shard_map/suffix/pallas_call | solution.py:334
  34.2 3.9 %all-to-all-done.1 = bf16[16,8,640]{2,1,0:T(8,128)(2,1)S(1)} async-done(((bf16[16,8,640]{2,1,0:T(8,128)(2,1)}), bf16[16,8,640]{2,1,0:T(8,128)(2,1)S(1)}, u32[]{:S(2)}, u32[]{:S(2)}) %all-to-all-start.1) | async-done | bytes 163872 | tf_op jit(solution)/shard_map/all_to_all | solution.py:390
  38.1 0.6 combine.1
  38.7 0.1 broadcast_in_dim.2
  38.9 19.4 %all_to_all.15 = bf16[16,32,1024]{2,1,0:T(8,128)(2,1)S(1)} all-to-all(bf16[16,32,1024]{2,1,0:T(8,128)(2,1)S(1)} %broadcast_in_dim.2), channel_id=1, replica_groups=mesh['owner'=16,'kv'=8] {'owner'}, dimensions={0} | all-to-all | bytes 2097152 | tf_op jit(solution)/shard_map/all_to_all | solution.py:410
  58.3 0.0 copy-done
  58.3 0.4 project_theirs.1
  58.7 0.1 collective-permute-start
  58.8 0.4 project_mine.1.mine_ref
  59.3 1.1 %collective-permute-done.other_ref = bf16[4,64,512]{2,1,0:T(8,128)(2,1)S(1)} collective-permute-done((bf16[4,64,512]{2,1,0:T(8,128)(2,1)S(1)}, bf16[4,64,512]{2,1,0:T(8,128)(2,1)S(1)}, u32[]{:S(2)}, u32[]{:S(2)}) %collective-permute-start) | collective-permute-done | bytes 262176 | tf_op jit(solution)/shard_map/ppermute | solution.py:429
  60.4 1.5 %collective-permute-start.1 = (bf16[64,512]{1,0:T(8,128)(2,1)S(1)}, bf16[64,512]{1,0:T(8,128)(2,1)S(1)}, u32[]{:S(2)}, u32[]{:S(2)}) collective-permute-start(bf16[64,512]{1,0:T(8,128)(2,1)S(1)} %get-tuple-element.22), channel_id=1, source_target_pairs={{0,2},{1,3},{2,4},{3,5},{4,6},{5,7},{6,0},{7,1},{8,10},{9,11},{10,... | collective-permute-start | bytes 196616 | tf_op jit(solution)/shard_map/ppermute | solution.py:443
  61.9 2.7 %collective-permute-start.2 = (bf16[64,512]{1,0:T(8,128)(2,1)S(1)}, bf16[64,512]{1,0:T(8,128)(2,1)S(1)}, u32[]{:S(2)}, u32[]{:S(2)}) collective-permute-start(bf16[64,512]{1,0:T(8,128)(2,1)S(1)} %get-tuple-element.23), channel_id=1, source_target_pairs={{0,4},{1,5},{2,6},{3,7},{4,0},{5,1},{6,2},{7,3},{8,12},{9,13},{10,... | collective-permute-start | bytes 196616 | tf_op jit(solution)/shard_map/ppermute | solution.py:443
  64.7 1.4 %collective-permute-start.3 = (bf16[64,512]{1,0:T(8,128)(2,1)S(1)}, bf16[64,512]{1,0:T(8,128)(2,1)S(1)}, u32[]{:S(2)}, u32[]{:S(2)}) collective-permute-start(bf16[64,512]{1,0:T(8,128)(2,1)S(1)} %get-tuple-element.24), channel_id=1, source_target_pairs={{0,6},{1,7},{2,0},{3,1},{4,2},{5,3},{6,4},{7,5},{8,14},{9,15},{10,... | collective-permute-start | bytes 196616 | tf_op jit(solution)/shard_map/ppermute | solution.py:443
  66.1 0.0 collective-permute-done.1
  66.1 2.1 %collective-permute-done.2 = bf16[64,512]{1,0:T(8,128)(2,1)S(1)} collective-permute-done((bf16[64,512]{1,0:T(8,128)(2,1)S(1)}, bf16[64,512]{1,0:T(8,128)(2,1)S(1)}, u32[]{:S(2)}, u32[]{:S(2)}) %collective-permute-start.2) | collective-permute-done | bytes 65568 | tf_op jit(solution)/shard_map/ppermute | solution.py:443
  68.2 0.8 %collective-permute-done.3 = bf16[64,512]{1,0:T(8,128)(2,1)S(1)} collective-permute-done((bf16[64,512]{1,0:T(8,128)(2,1)S(1)}, bf16[64,512]{1,0:T(8,128)(2,1)S(1)}, u32[]{:S(2)}, u32[]{:S(2)}) %collective-permute-start.3) | collective-permute-done | bytes 65568 | tf_op jit(solution)/shard_map/ppermute | solution.py:443
  68.9 0.7 add_convert_fusion
  (1 shorter events, 0.0 us)
Async XLA Ops:
  0.8 0.8 %copy-start.1 = (bf16[32,1024]{1,0:T(8,128)(2,1)S(1)}, bf16[32,1024]{1,0:T(8,128)(2,1)}, u32[]{:S(2)}) copy-start(bf16[32,1024]{1,0:T(8,128)(2,1)} %query_ref.1) | copy-start | bytes 196612
  2.7 16.1 %all-to-all-start = ((bf16[16,8,512]{2,1,0:T(8,128)(2,1)}), bf16[16,8,512]{2,1,0:T(8,128)(2,1)S(1)}, u32[]{:S(2)}, u32[]{:S(2)}) async-start(bf16[16,8,512]{2,1,0:T(8,128)(2,1)} %bitcast.2), calls=%async_computation | async-start | bytes 262144 | tf_op jit(solution)/shard_map/all_to_all | solution.py:322
  15.1 43.2 %copy-start = (bf16[1024,512]{1,0:T(8,128)(2,1)S(1)}, bf16[1024,512]{1,0:T(8,128)(2,1)}, u32[]{:S(2)}) copy-start(bf16[1024,512]{1,0:T(8,128)(2,1)} %weight_ref.3) | copy-start | bytes 3145732
  26.3 11.8 %all-to-all-start.1 = ((bf16[16,8,640]{2,1,0:T(8,128)(2,1)}), bf16[16,8,640]{2,1,0:T(8,128)(2,1)S(1)}, u32[]{:S(2)}, u32[]{:S(2)}) async-start(bf16[16,8,640]{2,1,0:T(8,128)(2,1)} %bitcast.6), calls=%async_computation.1 | async-start | bytes 327680 | tf_op jit(solution)/shard_map/all_to_all | solution.py:390
  58.7 1.6 %collective-permute-start = (bf16[4,64,512]{2,1,0:T(8,128)(2,1)S(1)}, bf16[4,64,512]{2,1,0:T(8,128)(2,1)S(1)}, u32[]{:S(2)}, u32[]{:S(2)}) collective-permute-start(bf16[4,64,512]{2,1,0:T(8,128)(2,1)S(1)} %project_theirs.1), channel_id=1, source_target_pairs={{0,1},{1,0},{2,3},{3,2},{4,5},{5,4},{6,7},{7,6},{8,9},{9,8},{10,11... | collective-permute-start | bytes 786440 | tf_op jit(solution)/shard_map/ppermute | solution.py:429
  60.4 5.7 %collective-permute-start.1 = (bf16[64,512]{1,0:T(8,128)(2,1)S(1)}, bf16[64,512]{1,0:T(8,128)(2,1)S(1)}, u32[]{:S(2)}, u32[]{:S(2)}) collective-permute-start(bf16[64,512]{1,0:T(8,128)(2,1)S(1)} %get-tuple-element.22), channel_id=1, source_target_pairs={{0,2},{1,3},{2,4},{3,5},{4,6},{5,7},{6,0},{7,1},{8,10},{9,11},{10,... | collective-permute-start | bytes 196616 | tf_op jit(solution)/shard_map/ppermute | solution.py:443
  61.9 6.3 %collective-permute-start.2 = (bf16[64,512]{1,0:T(8,128)(2,1)S(1)}, bf16[64,512]{1,0:T(8,128)(2,1)S(1)}, u32[]{:S(2)}, u32[]{:S(2)}) collective-permute-start(bf16[64,512]{1,0:T(8,128)(2,1)S(1)} %get-tuple-element.23), channel_id=1, source_target_pairs={{0,4},{1,5},{2,6},{3,7},{4,0},{5,1},{6,2},{7,3},{8,12},{9,13},{10,... | collective-permute-start | bytes 196616 | tf_op jit(solution)/shard_map/ppermute | solution.py:443
  64.7 4.3 %collective-permute-start.3 = (bf16[64,512]{1,0:T(8,128)(2,1)S(1)}, bf16[64,512]{1,0:T(8,128)(2,1)S(1)}, u32[]{:S(2)}, u32[]{:S(2)}) collective-permute-start(bf16[64,512]{1,0:T(8,128)(2,1)S(1)} %get-tuple-element.24), channel_id=1, source_target_pairs={{0,6},{1,7},{2,0},{3,1},{4,2},{5,3},{6,4},{7,5},{8,14},{9,15},{10,... | collective-permute-start | bytes 196616 | tf_op jit(solution)/shard_map/ppermute | solution.py:443
